TPU v7x, 32 devices: a whole 2x2x4 slice. The times are simulated.
32 devices in a mesh: row: 8 (over z, x), col: 4 (over y, core).
Axes of the slice: x: 2, y: 2, z: 4, core: 2. Of those that a mesh axis runs over, the one named last changes fastest.
Arguments:
- panel_block: float32 [16384, 128], P('row'), may hold values from -8 to 8, as said below
- trailing: float32 [16384, 16384], P('row', 'col'), may hold values from -80 to 80
Outputs:
- reduced: float32 [16384, 16384], P('row', 'col')
- band_block: float32 [128, 128], replicated
- first_factor: float32 [128, 128], replicated
Inputs may be any that keep to these rules, and one draw needn't show every extreme that they name: `panel_block`: entries of order the inverse square root of 16384; rows may differ in scale; the columns may be nearly dependent, with a condition number of the panel up to a few thousand; the first 128 rows of the orthonormal basis have spectral norm at most 0.8, so that I + top^T needs no pivoting.
All inputs are finite; a program needn't handle non-finite values.
Results may differ from a plain program's by a relative error of at most 0.0017.
Values sent between devices are 32-bit elements; how exact they have to be, the bound alone decides.
No kernel may reach another device: no remote copies, remote signals or barrier semaphores. Data moves between devices by JAX's collectives and lax.ppermute only.
A program may use at most 128 MiB of HBM per device.

v0:
```python
import functools

import jax
import jax.numpy as jnp
from jax import lax
from jax.experimental import pallas as pl
from jax.experimental.pallas import tpu as pltpu
from jax.sharding import PartitionSpec as P

HIGH = lax.Precision.HIGHEST
F32 = jnp.float32
BF16 = jnp.bfloat16
SUB = 8


def dot_nn(a, b):
    return lax.dot_general(a, b, (((1,), (0,)), ((), ())), precision=HIGH, preferred_element_type=F32)


def dot_nt(a, b):
    return lax.dot_general(a, b, (((1,), (1,)), ((), ())), precision=HIGH, preferred_element_type=F32)


def dot_tn(a, b):
    return lax.dot_general(a, b, (((0,), (0,)), ((), ())), precision=HIGH, preferred_element_type=F32)


def dot_fast(a, b):
    return lax.dot_general(a, b, (((1,), (0,)), ((), ())), preferred_element_type=F32)


def lane_copy(tile, lane):
    return jnp.broadcast_to(tile[:, lane : lane + 1], tile.shape)


def row_copy(tile, row):
    return jnp.broadcast_to(tile[row : row + 1, :], tile.shape)


def cholesky_tiles(tiles):
    size = tiles[0].shape[1]
    count = len(tiles)
    tiles = list(tiles)
    lanes = lax.broadcasted_iota(jnp.int32, (SUB, size), 1)
    subs = lax.broadcasted_iota(jnp.int32, (SUB, size), 0)
    upper, inverse = [], []
    for block in range(count):
        base = block * SUB
        here = (lanes >= base) & (lanes < base + SUB)
        columns = [[lane_copy(tiles[i], base + k) for k in range(SUB)] for i in range(block, count)]
        right = jnp.where(lanes >= base, tiles[block], 0.0)
        left = jnp.where(lanes < base, tiles[block], 0.0)
        left = jnp.where(lanes - base == subs, 1.0, left)
        out_upper, out_inverse = jnp.zeros_like(right), jnp.zeros_like(left)
        below = [jnp.where(here, 0.0, tiles[i]) for i in range(block + 1, count)]
        for k in range(SUB):
            diag = columns[0]
            pivot = row_copy(diag[k], k)
            root = lax.rsqrt(pivot)
            recip = 1.0 / pivot
            right_row, left_row = row_copy(right, k), row_copy(left, k)
            out_upper = jnp.where(subs == k, right_row * root, out_upper)
            out_inverse = jnp.where(subs == k, left_row * root, out_inverse)
            packed = jnp.where(lanes < base + SUB, left_row, right_row) * recip
            rows = {l: row_copy(diag[l], k) * recip for l in range(k + 1, SUB)}
            factor = jnp.where(subs > k, diag[k], 0.0)
            right = right - factor * (right_row * recip)
            left = left - factor * (left_row * recip)
            for i in range(count - block):
                for l in range(k + 1, SUB):
                    if i == 0:
                        columns[0][l] = columns[0][l] - factor * rows[l]
                    else:
                        columns[i][l] = columns[i][l] - columns[i][k] * rows[l]
                if i:
                    below[i - 1] = below[i - 1] - columns[i][k] * packed
        for i in range(block + 1, count):
            tiles[i] = below[i - block - 1]
        upper.append(jnp.where(lanes >= base + subs, out_upper, 0.0))
        inverse.append(out_inverse)
    return upper, inverse


def invert_tiles(tiles):
    size = tiles[0].shape[1]
    count = len(tiles)
    tiles = list(tiles)
    lanes = lax.broadcasted_iota(jnp.int32, (SUB, size), 1)
    subs = lax.broadcasted_iota(jnp.int32, (SUB, size), 0)
    for block in range(count):
        base = block * SUB
        here = (lanes >= base) & (lanes < base + SUB)
        columns = [[lane_copy(tiles[i], base + k) for k in range(SUB)] for i in range(count)]
        diag = list(columns[block])
        row = jnp.where(here, jnp.where(lanes - base == subs, 1.0, 0.0), tiles[block])
        for k in range(SUB):
            recip = 1.0 / row_copy(diag[k], k)
            own = subs == k
            pivot_row = row_copy(row, k) * recip
            rows = {l: row_copy(diag[l], k) * recip for l in range(k + 1, SUB)}
            row = jnp.where(own, pivot_row, row - diag[k] * pivot_row)
            for l in range(k + 1, SUB):
                diag[l] = jnp.where(own, rows[l], diag[l] - diag[k] * rows[l])
        spread = [row_copy(row, k) for k in range(SUB)]
        for i in range(count):
            if i == block:
                continue
            value = jnp.where(here, 0.0, tiles[i])
            for k in range(SUB):
                value = value - columns[i][k] * spread[k]
            tiles[i] = value
        tiles[block] = row
    return tiles


def tiles_of(ref):
    return [ref[i * SUB : (i + 1) * SUB, :] for i in range(ref.shape[0] // SUB)]


def first_kernel(gram_ref, panel_ref, factor_ref, inverse_ref, basis_ref, second_ref):
    upper, inverse = cholesky_tiles(tiles_of(gram_ref))
    factor_ref[...] = jnp.concatenate(upper, axis=0).T
    inverse_ref[...] = jnp.concatenate(inverse, axis=0)
    basis_ref[...] = dot_nt(panel_ref[...], inverse_ref[...])
    basis = basis_ref[...]
    second_ref[...] = dot_tn(basis, basis)


def first_pass(gram, panel):
    square = jax.ShapeDtypeStruct(gram.shape, F32)
    return pl.pallas_call(
        first_kernel,
        out_shape=(square, square, jax.ShapeDtypeStruct(panel.shape, F32), square),
        compiler_params=pltpu.CompilerParams(vmem_limit_bytes=24 * 1024 * 1024),
        name="first_pass",
    )(gram, panel)


def second_kernel(gram_ref, upper_ref, inverse_ref):
    upper, inverse = cholesky_tiles(tiles_of(gram_ref))
    upper_ref[...] = jnp.concatenate(upper, axis=0)
    inverse_ref[...] = jnp.concatenate(inverse, axis=0)


def second_pass(gram):
    square = jax.ShapeDtypeStruct(gram.shape, F32)
    return pl.pallas_call(
        second_kernel,
        out_shape=(square, square),
        compiler_params=pltpu.CompilerParams(vmem_limit_bytes=8 * 1024 * 1024),
        name="second_pass",
    )(gram)


def small_kernel(upper_ref, inverse_ref, first_ref, top_ref, band_ref, kernel_ref):
    band_ref[...] = -dot_nt(upper_ref[...], first_ref[...])
    size = upper_ref.shape[0]
    rows = lax.broadcasted_iota(jnp.int32, (size, size), 0)
    lanes = lax.broadcasted_iota(jnp.int32, (size, size), 1)
    eye = jnp.where(rows == lanes, 1.0, 0.0)
    kernel_ref[...] = eye + dot_nt(inverse_ref[...], top_ref[...])
    kernel_ref[...] = jnp.concatenate(invert_tiles(tiles_of(kernel_ref)), axis=0)


def small_pass(upper, inverse, first_factor, top):
    square = jax.ShapeDtypeStruct(upper.shape, F32)
    return pl.pallas_call(
        small_kernel,
        out_shape=(square, square),
        compiler_params=pltpu.CompilerParams(vmem_limit_bytes=8 * 1024 * 1024),
        name="small_pass",
    )(upper, inverse, first_factor, top)


def split(value):
    high = value.astype(BF16)
    return high, (value - high.astype(F32)).astype(BF16)


def fetch(away, holder, other, into, sem):
    @pl.when(away == 0)
    def _():
        copy = pltpu.make_async_copy(holder, into, sem)
        copy.start()
        copy.wait()

    @pl.when(away != 0)
    def _():
        copy = pltpu.make_async_copy(other, into, sem)
        copy.start()
        copy.wait()


def chunk_of(rows):
    return min(rows, 256)


def product_kernel(
    index_ref, trailing, inverse_ref, before_ref, holder_ref, other_ref,
    out_ref, basis_ref, tiles, panel, both, sem, sems,
):
    slots, chunk, depth = tiles.shape
    rows, width = out_ref.shape
    count = rows // chunk
    columns = pl.ds(pl.multiple_of(index_ref[0] * depth, depth), depth)

    def load(i):
        part = pl.ds(pl.multiple_of(i * chunk, chunk), chunk)
        slot = i % slots
        return pltpu.make_async_copy(trailing.at[part, columns], tiles.at[slot], sems.at[slot])

    for i in range(slots):
        load(i).start()

    fetch(index_ref[1], holder_ref, other_ref, panel, sem)
    basis_ref[...] = dot_nt(panel[...], inverse_ref[...])
    high, low = split(basis_ref[...])
    both[:, :width] = high
    both[:, width:] = low

    @pl.loop(0, rows // chunk)
    def _(i):
        load(i).wait()
        part = pl.ds(pl.multiple_of(i * chunk, chunk), chunk)
        high, low = split(tiles[i % slots])
        right = both[...]
        value = dot_fast(high, right) + dot_fast(low, right)
        out_ref[part, :] = before_ref[part, :] + (value[:, :width] + value[:, width:])

        @pl.when(i + slots < count)
        def _():
            load(i + slots).start()


def product(index, trailing, inverse, before, holder, other):
    rows = trailing.shape[0]
    depth, width = holder.shape
    chunk = chunk_of(rows)
    slots = min(4, rows // chunk)
    anywhere = pl.BlockSpec(memory_space=pl.ANY)
    near = pl.BlockSpec(memory_space=pltpu.VMEM)
    return pl.pallas_call(
        product_kernel,
        out_shape=(
            jax.ShapeDtypeStruct((rows, width), F32),
            jax.ShapeDtypeStruct((depth, width), F32),
        ),
        in_specs=[
            pl.BlockSpec(memory_space=pltpu.SMEM),
            anywhere,
            near,
            near,
            anywhere,
            anywhere,
        ],
        out_specs=(near, near),
        scratch_shapes=[
            pltpu.VMEM((slots, chunk, depth), F32),
            pltpu.VMEM((depth, width), F32),
            pltpu.VMEM((depth, 2 * width), BF16),
            pltpu.SemaphoreType.DMA,
            pltpu.SemaphoreType.DMA((slots,)),
        ],
        compiler_params=pltpu.CompilerParams(vmem_limit_bytes=20 * 1024 * 1024),
        cost_estimate=pl.CostEstimate(
            flops=8 * rows * depth * width, bytes_accessed=4 * rows * depth, transcendentals=0
        ),
        name="product",
    )(index, trailing, inverse, before, holder, other)


def update_kernel(
    index_ref, trailing, left_ref, vectors_ref, holder_ref, other_ref, _,
    out, tiles, applied, right, sem, loads, stores,
):
    slots, chunk, depth = tiles.shape
    rows, width = left_ref.shape[0], vectors_ref.shape[1]
    count = rows // chunk
    ahead = max(slots - 2, 1)
    columns = pl.ds(pl.multiple_of(index_ref[0] * depth, depth), depth)

    def load(i):
        part = pl.ds(pl.multiple_of(i * chunk, chunk), chunk)
        slot = i % slots
        return pltpu.make_async_copy(trailing.at[part, columns], tiles.at[slot], loads.at[slot])

    def store(i):
        part = pl.ds(pl.multiple_of(i * chunk, chunk), chunk)
        slot = i % slots
        return pltpu.make_async_copy(tiles.at[slot], out.at[part, columns], stores.at[slot])

    for i in range(min(ahead, count)):
        load(i).start()

    fetch(index_ref[1], holder_ref, other_ref, applied, sem)
    for place, ref in ((0, applied), (width, vectors_ref)):
        high, low = split(ref[...].T)
        right[place : place + width, :] = high
        right[2 * width + place : 3 * width + place, :] = low
        right[4 * width + place : 5 * width + place, :] = high

    @pl.loop(0, count)
    def _(i):
        @pl.when(i + ahead < count)
        def _():
            @pl.when(i + ahead >= slots)
            def _():
                store(i + ahead - slots).wait()

            load(i + ahead).start()

        load(i).wait()
        part = pl.ds(pl.multiple_of(i * chunk, chunk), chunk)
        high, low = split(left_ref[part, :])
        left = jnp.concatenate([high, high, low], axis=1)
        slot = i % slots
        tiles[slot] = tiles[slot] - dot_fast(left, right[...])
        store(i).start()

    for i in range(max(count - slots, 0), count):
        store(i).wait()


def update(index, trailing, left, vectors, holder, other, reduced):
    rows = trailing.shape[0]
    depth, width = vectors.shape
    chunk = chunk_of(rows)
    slots = min(5, rows // chunk)
    anywhere = pl.BlockSpec(memory_space=pl.ANY)
    near = pl.BlockSpec(memory_space=pltpu.VMEM)
    aliases = {}
    if reduced is None:
        reduced = index
    else:
        aliases = {6: 0}
    return pl.pallas_call(
        update_kernel,
        out_shape=jax.ShapeDtypeStruct(trailing.shape, F32),
        in_specs=[
            pl.BlockSpec(memory_space=pltpu.SMEM),
            anywhere,
            near,
            near,
            anywhere,
            anywhere,
            anywhere,
        ],
        out_specs=anywhere,
        scratch_shapes=[
            pltpu.VMEM((slots, chunk, depth), F32),
            pltpu.VMEM((depth, width), F32),
            pltpu.VMEM((6 * width, depth), BF16),
            pltpu.SemaphoreType.DMA,
            pltpu.SemaphoreType.DMA((slots,)),
            pltpu.SemaphoreType.DMA((slots,)),
        ],
        input_output_aliases=aliases,
        compiler_params=pltpu.CompilerParams(vmem_limit_bytes=26 * 1024 * 1024),
        cost_estimate=pl.CostEstimate(
            flops=12 * rows * depth * width, bytes_accessed=8 * rows * depth, transcendentals=0
        ),
        name="update",
    )(index, trailing, left, vectors, holder, other, reduced)


def dot_three(a, b, dims):
    a_high, a_low = split(a)
    b_high, b_low = split(b)
    dot = lambda x, y: lax.dot_general(x, y, (dims, ((), ())), preferred_element_type=F32)
    return dot(a_high, b_high) + (dot(a_high, b_low) + dot(a_low, b_high))


def applied_kernel(
    index_ref, raw_ref, basis_ref, inverse_ref, lead_ref, give_ref, keep_ref, vectors_ref, inner_ref
):
    step = pl.program_id(0)
    half, width = raw_ref.shape
    value = dot_three(raw_ref[...], inverse_ref[...], ((1,), (1,)))
    value = value + jnp.where(index_ref[1] == 0, lead_ref[...], 0.0)
    first = index_ref[2] + (1 - (index_ref[0] ^ step)) * half
    rows = lax.broadcasted_iota(jnp.int32, (half, width), 0) + first
    lanes = lax.broadcasted_iota(jnp.int32, (half, width), 1)
    vectors = dot_three(basis_ref[...], inverse_ref[...], ((1,), (1,)))
    vectors = vectors + jnp.where(rows == lanes, 1.0, 0.0)
    vectors_ref[...] = vectors
    inner = dot_three(vectors, value, ((0,), (0,)))

    @pl.when(step == 0)
    def _():
        give_ref[...] = value
        inner_ref[...] = inner

    @pl.when(step == 1)
    def _():
        keep_ref[...] = value
        inner_ref[...] += inner


def applied_halves(index, raw, basis, inverse, trailing):
    rows, width = raw.shape
    half = rows // 2
    whole = pl.BlockSpec((half, width), lambda i, index: (0, 0))
    square = pl.BlockSpec((width, width), lambda i, index: (0, 0))
    piece = pl.BlockSpec((half, width), lambda i, index: (1 - (index[0] ^ i), 0))
    out = jax.ShapeDtypeStruct((half, width), F32)
    return pl.pallas_call(
        applied_kernel,
        out_shape=(
            out,
            out,
            jax.ShapeDtypeStruct((rows, width), F32),
            jax.ShapeDtypeStruct((width, width), F32),
        ),
        grid_spec=pltpu.PrefetchScalarGridSpec(
            num_scalar_prefetch=1,
            grid=(2,),
            in_specs=[piece, piece, square, piece],
            out_specs=(whole, whole, piece, square),
        ),
        compiler_params=pltpu.CompilerParams(vmem_limit_bytes=24 * 1024 * 1024),
        name="applied",
    )(index, raw, basis, inverse, trailing)


def after(value, *others):
    return lax.optimization_barrier((value, *others))[0]


def swap(value, axis, bit):
    count = lax.axis_size(axis)
    return lax.ppermute(value, axis, [(i, i ^ bit) for i in range(count)])


def bits_of(count):
    return [1 << b for b in range(count.bit_length() - 1)]


def sum_small(value, axis, bits):
    for bit in bits:
        value = value + swap(value, axis, bit)
    return value


class Gather:
    def __init__(self):
        self.row_n, self.col_n = lax.axis_size("row"), lax.axis_size("col")
        self.ratio = self.row_n // self.col_n
        self.away = (lax.axis_index("row") // self.ratio) ^ lax.axis_index("col")

    def move(self, value, holds, to_row):
        pairs = []
        for r in range(self.row_n):
            for c in range(self.col_n):
                if holds((r // self.ratio) ^ c):
                    pairs.append((r * self.col_n + c, to_row(r) * self.col_n + c))
        return lax.ppermute(value, ("row", "col"), pairs)

    def relay(self, value, done=0):
        for bit in reversed(bits_of(self.col_n)[1:]):
            if bit & done:
                continue
            moved = self.move(
                value, lambda d: d & ~done == 0, lambda r: r ^ (bit * self.ratio)
            )
            value = jnp.where((self.away & ~done) == bit, moved, value)
            done |= bit
        return value

    def relay_halves(self, value, meanwhile):
        bit = self.col_n // 2
        half = value.shape[0] // 2
        across = (self.away == bit).astype(jnp.int32)
        piece = lax.dynamic_slice_in_dim(value, across * half, half, 0)
        first = self.move(piece, lambda d: d & ~bit == 0, lambda r: r ^ (bit * self.ratio))
        first, meanwhile = lax.optimization_barrier((first, meanwhile))
        pairs = []
        for r in range(self.row_n):
            c = r // self.ratio
            pairs.append((r * self.col_n + c, r * self.col_n + (c ^ bit)))
        second = lax.ppermute(first, ("row", "col"), pairs)
        moved = jnp.concatenate([first, second])
        return jnp.where(self.away == bit, moved, value), meanwhile

    def near(self, value):
        holds = lambda d: d & 1 == 0
        return (
            self.move(value, holds, lambda r: r ^ self.ratio),
            self.move(value, holds, lambda r: r ^ 1),
        )

    def across(self, moved_high):
        return self.move(moved_high, lambda d: d & 1 == 1, lambda r: r ^ 1)

    def rest(self, blocks):
        full = []
        for holder, other in blocks:
            full.append(jnp.where(self.away & 1 == 0, holder, other))
        for bit in bits_of(self.ratio)[1:]:
            full += [swap(value, "row", bit) for value in full]
        return [(value, value) for value in full[2:]]


def broadcast_col(value):
    col_n = lax.axis_size("col")
    col = lax.axis_index("col")
    for bit in bits_of(col_n):
        moved = lax.ppermute(value, "col", [(i, i + bit) for i in range(bit)])
        value = jnp.where((col >= bit) & (col < 2 * bit), moved, value)
    return value


def body(panel_block, trailing):
    shard_rows, width = panel_block.shape
    half = shard_rows // 2
    row, col = lax.axis_index("row"), lax.axis_index("col")
    row_bits, col_bits = bits_of(lax.axis_size("row")), bits_of(lax.axis_size("col"))
    gather = Gather()
    ratio = gather.ratio
    low = row % ratio
    lane = jnp.arange(width)

    def identity_rows(first):
        return ((first + jnp.arange(shard_rows))[:, None] == lane).astype(F32)

    def index_of(part):
        return jnp.stack([part ^ low, gather.away & 1]).astype(jnp.int32)

    gram = sum_small(dot_tn(panel_block, panel_block), "row", row_bits[:1])
    relayed, gram = gather.relay_halves(panel_block, gram)
    relayed = gather.relay(relayed, lax.axis_size("col") // 2)
    gram = sum_small(gram, "row", row_bits[1:])
    moved_high, moved_low = gather.near(after(relayed, gram))
    first_factor, first_inverse, first_basis, second = first_pass(gram, panel_block)

    moved_high, second = lax.optimization_barrier((moved_high, second))
    parts = [(relayed, moved_high), (moved_low, gather.across(moved_high))]
    raw, basis = product(
        index_of(0), trailing, first_inverse, jnp.zeros((shard_rows, width), F32), *parts[0]
    )
    bases = [basis]
    second = sum_small(second, "row", row_bits[::-1])
    parts += gather.rest(parts)
    for part in range(1, ratio):
        raw, basis = product(index_of(part), trailing, first_inverse, raw, *parts[part])
        bases.append(basis)
    second_upper, second_inverse = second_pass(second)

    mine = col & 1
    give, keep, vectors, inner = applied_halves(
        jnp.stack([mine, col, row * shard_rows]).astype(jnp.int32),
        raw,
        first_basis,
        second_inverse,
        trailing,
    )
    keep = keep + swap(give, "col", col_bits[0])
    inner = sum_small(inner, "row", row_bits)
    for bit in col_bits[1:]:
        moved, inner = lax.optimization_barrier((swap(keep, "col", bit), inner))
        keep = keep + moved
    other = swap(keep, "col", col_bits[0])
    applied = jnp.zeros((shard_rows, width), F32)
    applied = lax.dynamic_update_slice_in_dim(applied, keep, mine * half, 0)
    applied = lax.dynamic_update_slice_in_dim(applied, other, (1 - mine) * half, 0)

    relayed = gather.relay(applied)
    inner = sum_small(inner, "col", col_bits)
    top = sum(jnp.where(low == part, basis[:width], 0.0) for part, basis in enumerate(bases))
    top = broadcast_col(after(top, applied))
    band_block, kernel = small_pass(second_upper, second_inverse, first_factor, top)
    inner = dot_tn(kernel, dot_nn(inner, kernel))
    left = jnp.concatenate(
        [dot_nt(vectors, kernel), dot_nn(applied, kernel) - dot_nn(vectors, inner)], axis=1
    )
    block_vectors = [
        dot_nt(basis, second_inverse) + identity_rows((col * ratio + (part ^ low)) * shard_rows)
        for part, basis in enumerate(bases)
    ]
    moved_high, moved_low = gather.near(relayed)
    parts = [(relayed, moved_high), (moved_low, gather.across(moved_high))]
    reduced = update(index_of(0), trailing, left, block_vectors[0], *parts[0], None)
    parts += gather.rest(parts)
    for part in range(1, ratio):
        reduced = update(index_of(part), trailing, left, block_vectors[part], *parts[part], reduced)
    return (reduced, band_block, first_factor)


def solution(mesh):
    in_specs = (P("row", None), P("row", "col"))
    out_specs = (P("row", "col"), P(), P())
    return jax.shard_map(body, mesh=mesh, in_specs=in_specs, out_specs=out_specs, check_vma=False)
```

profile of v0, /device:TPU:6, one launch (start us, length us, event | category | flops | bytes accessed | tf_op | source)
XLA Modules:
  0.0 195.0 jit_solution(385614764267535876)
XLA Ops:
  1.8 4.5 %collective-permute-start = (f32[1024,128]{1,0:T(8,128)S(1)}, f32[1024,128]{1,0:T(8,128)S(1)}, u32[]{:S(2)}, u32[]{:S(2)}) collective-permute-start(f32[1024,128]{1,0:T(8,128)S(1)} %constant_dynamic-slice_fusion), channel_id=1, source_target_pairs={{0,16},{2,18},{4,20},{6,22},{9,25},{11,27},{13,29},{15,31},{16,0},... | collective-permute-start | bytes 1572872 | tf_op jit(solution)/shard_map/ppermute | solution.py:456
  8.8 3.7 %collective-permute-done.1 = f32[128,128]{1,0:T(8,128)S(1)} collective-permute-done((f32[128,128]{1,0:T(8,128)S(1)}, f32[128,128]{1,0:T(8,128)S(1)}, u32[]{:S(2)}, u32[]{:S(2)}) %collective-permute-start.1) | collective-permute-done | bytes 65568 | tf_op jit(solution)/shard_map/ppermute | solution.py:431
  12.5 6.8 %collective-permute-done = f32[1024,128]{1,0:T(8,128)S(1)} collective-permute-done((f32[1024,128]{1,0:T(8,128)S(1)}, f32[1024,128]{1,0:T(8,128)S(1)}, u32[]{:S(2)}, u32[]{:S(2)}) %collective-permute-start) | collective-permute-done | bytes 524320 | tf_op jit(solution)/shard_map/ppermute | solution.py:456
  20.7 4.3 %collective-permute-done.2 = f32[128,128]{1,0:T(8,128)S(1)} collective-permute-done((f32[128,128]{1,0:T(8,128)S(1)}, f32[128,128]{1,0:T(8,128)S(1)}, u32[]{:S(2)}, u32[]{:S(2)}) %collective-permute-start.2) | collective-permute-done | bytes 65568 | tf_op jit(solution)/shard_map/ppermute | solution.py:431
  26.0 4.3 %collective-permute-done.3 = f32[128,128]{1,0:T(8,128)S(1)} collective-permute-done((f32[128,128]{1,0:T(8,128)S(1)}, f32[128,128]{1,0:T(8,128)S(1)}, u32[]{:S(2)}, u32[]{:S(2)}) %collective-permute-start.3) | collective-permute-done | bytes 65568 | tf_op jit(solution)/shard_map/ppermute | solution.py:431
  30.5 2.7 %collective-permute-start.5 = (f32[2048,128]{1,0:T(8,128)S(1)}, f32[2048,128]{1,0:T(8,128)}, u32[]{:S(2)}, u32[]{:S(2)}) collective-permute-start(f32[2048,128]{1,0:T(8,128)S(1)} %maximum_select_fusion.holder_ref), channel_id=1, source_target_pairs={{0,8},{2,10},{4,12},{6,14},{9,1},{11,3},{13,5},{15,7},{16,24},{18,... | collective-permute-start | bytes 3145736 | tf_op jit(solution)/shard_map/ppermute | solution.py:456
  33.2 7.9 %first_pass.1 = (f32[128,128]{1,0:T(8,128)}, f32[128,128]{1,0:T(8,128)S(1)}, f32[2048,128]{1,0:T(8,128)S(1)}, f32[128,128]{1,0:T(8,128)S(1)}) custom-call(f32[128,128]{1,0:T(8,128)S(1)} %add.89.gram_ref, f32[2048,128]{1,0:T(8,128)S(1)} %copy-done), custom_call_target="tpu_custom_call" | custom-call | tf_op jit(solution)/shard_map/first_pass/pallas_call | solution.py:131
  47.0 4.4 %collective-permute-done.8 = f32[128,128]{1,0:T(8,128)S(1)} collective-permute-done((f32[128,128]{1,0:T(8,128)S(1)}, f32[128,128]{1,0:T(8,128)S(1)}, u32[]{:S(2)}, u32[]{:S(2)}) %collective-permute-start.8) | collective-permute-done | bytes 65568 | tf_op jit(solution)/shard_map/ppermute | solution.py:431
  51.5 3.4 %collective-permute-start.9 = (f32[128,128]{1,0:T(8,128)S(1)}, f32[128,128]{1,0:T(8,128)S(1)}, u32[]{:S(2)}, u32[]{:S(2)}) collective-permute-start(f32[128,128]{1,0:T(8,128)S(1)} %add.90), channel_id=1, source_target_pairs={{0,8},{4,12},{8,0},{12,4},{16,24},{20,28},{24,16},{28,20},{1,9},{5... | collective-permute-start | bytes 196616 | tf_op jit(solution)/shard_map/ppermute | solution.py:431
  58.8 7.9 %product.2 = (f32[2048,128]{1,0:T(8,128)S(1)}, f32[2048,128]{1,0:T(8,128)S(1)}) custom-call(s32[2]{0:T(128)S(1)} %pad_add_fusion.2.index_ref._, f32[2048,4096]{1,0:T(8,128)} %trailing.7, f32[128,128]{1,0:T(8,128)S(1)} %get-tuple-element.28.inverse_ref, f32[2048,128]{1,0:T(8,128)S(1)} %broadcast_1_before_ref.2.before_ref, ...), custom_call_target="tpu_custom_call" | custom-call | flops 4294967296 | bytes 16777216 | tf_op jit(solution)/shard_map/product/pallas_call | solution.py:242
  66.7 4.2 %collective-permute-done.10 = f32[128,128]{1,0:T(8,128)S(1)} collective-permute-done((f32[128,128]{1,0:T(8,128)S(1)}, f32[128,128]{1,0:T(8,128)S(1)}, u32[]{:S(2)}, u32[]{:S(2)}) %collective-permute-start.10) | collective-permute-done | bytes 65568 | tf_op jit(solution)/shard_map/ppermute | solution.py:431
  71.0 4.1 %second_pass.1 = (f32[128,128]{1,0:T(8,128)S(1)}, f32[128,128]{1,0:T(8,128)S(1)}) custom-call(f32[128,128]{1,0:T(8,128)S(1)} %add.92.gram_ref), custom_call_target="tpu_custom_call" | custom-call | tf_op jit(solution)/shard_map/second_pass/pallas_call | solution.py:147
  75.1 11.0 %product.3 = (f32[2048,128]{1,0:T(8,128)S(1)}, f32[2048,128]{1,0:T(8,128)S(1)}) custom-call(s32[2]{0:T(128)S(1)} %pad_add_fusion.index_ref, f32[2048,4096]{1,0:T(8,128)} %trailing.7, f32[128,128]{1,0:T(8,128)S(1)} %get-tuple-element.28.inverse_ref, f32[2048,128]{1,0:T(8,128)S(1)} %get-tuple-element.33.before_ref, ...), custom_call_target="tpu_custom_call" | custom-call | flops 4294967296 | bytes 16777216 | tf_op jit(solution)/shard_map/product/pallas_call | solution.py:242
  87.0 3.6 %applied.1 = (f32[1024,128]{1,0:T(8,128)S(1)}, f32[1024,128]{1,0:T(8,128)S(1)}, f32[2048,128]{1,0:T(8,128)S(1)}, f32[128,128]{1,0:T(8,128)S(1)}) custom-call(s32[3]{0:T(128)S(1)} %pad_add_fusion.1.index_ref, f32[2048,128]{1,0:T(8,128)S(1)} %get-tuple-element.34.raw_ref, f32[2048,128]{1,0:T(8,128)S(1)} %copy-done.4, ...), custom_call_target="tpu_custom_call" | custom-call | tf_op jit(solution)/shard_map/applied/pallas_call | solution.py:406
  95.8 3.7 %collective-permute-done.13 = f32[128,128]{1,0:T(8,128)S(1)} collective-permute-done((f32[128,128]{1,0:T(8,128)S(1)}, f32[128,128]{1,0:T(8,128)S(1)}, u32[]{:S(2)}, u32[]{:S(2)}) %collective-permute-start.13) | collective-permute-done | bytes 65568 | tf_op jit(solution)/shard_map/ppermute | solution.py:431
  101.4 2.5 %collective-permute-done.14 = f32[128,128]{1,0:T(8,128)S(1)} collective-permute-done((f32[128,128]{1,0:T(8,128)S(1)}, f32[128,128]{1,0:T(8,128)S(1)}, u32[]{:S(2)}, u32[]{:S(2)}) %collective-permute-start.14) | collective-permute-done | bytes 65568 | tf_op jit(solution)/shard_map/ppermute | solution.py:431
  104.9 4.3 %collective-permute-done.15 = f32[128,128]{1,0:T(8,128)S(1)} collective-permute-done((f32[128,128]{1,0:T(8,128)S(1)}, f32[128,128]{1,0:T(8,128)S(1)}, u32[]{:S(2)}, u32[]{:S(2)}) %collective-permute-start.15) | collective-permute-done | bytes 65568 | tf_op jit(solution)/shard_map/ppermute | solution.py:431
  119.4 4.4 %collective-permute-start.20 = (f32[128,128]{1,0:T(8,128)S(1)}, f32[128,128]{1,0:T(8,128)S(1)}, u32[]{:S(2)}, u32[]{:S(2)}) collective-permute-start(f32[128,128]{1,0:T(8,128)S(1)} %add.101), channel_id=1, source_target_pairs={{0,2},{1,3},{2,0},{3,1},{4,6},{5,7},{6,4},{7,5},{8,10},{9,11},{10,... | collective-permute-start | bytes 196616 | tf_op jit(solution)/shard_map/ppermute | solution.py:431
  125.1 18.5 %collective-permute-done.21 = f32[2048,128]{1,0:T(8,128)} collective-permute-done((f32[2048,128]{1,0:T(8,128)S(1)}, f32[2048,128]{1,0:T(8,128)}, u32[]{:S(2)}, u32[]{:S(2)}) %collective-permute-start.21) | collective-permute-done | bytes 1048608 | tf_op jit(solution)/shard_map/ppermute | solution.py:456
  146.6 7.0 %small_pass.1 = (f32[128,128]{1,0:T(8,128)}, f32[128,128]{1,0:T(8,128)S(1)}) custom-call(f32[128,128]{1,0:T(8,128)S(1)} %get-tuple-element.39.upper_ref, f32[128,128]{1,0:T(8,128)S(1)} %get-tuple-element.37.inverse_ref, f32[128,128]{1,0:T(8,128)S(1)} %copy-done.5, f32[128,128]{1,0:T(8,128)S(1)} %broadcast_select_fusion.2.top_ref), custom_call_target="tpu_custom_call" | custom-call | tf_op jit(solution)/shard_map/small_pass/pallas_call | solution.py:167
  156.1 2.4 %collective-permute-start.22 = (f32[2048,128]{1,0:T(8,128)S(1)}, f32[2048,128]{1,0:T(8,128)S(1)}, u32[]{:S(2)}, u32[]{:S(2)}) collective-permute-start(f32[2048,128]{1,0:T(8,128)S(1)} %broadcast_select_fusion.holder_ref), channel_id=1, source_target_pairs={{0,4},{2,6},{4,0},{6,2},{9,13},{11,15},{13,9},{15,11},{16,20},{18,... | collective-permute-start | bytes 3145736 | tf_op jit(solution)/shard_map/ppermute | solution.py:456
  160.6 13.4 %update.2._ = f32[2048,4096]{1,0:T(8,128)} custom-call(s32[2]{0:T(128)S(1)} %pad_add_fusion.2.index_ref._, f32[2048,4096]{1,0:T(8,128)} %trailing.7, f32[2048,256]{1,0:T(8,128)S(1)} %pad_maximum_fusion.left_ref, f32[2048,128]{1,0:T(8,128)S(1)} %convolution_add_fusion.vectors_ref, f32[2048,128]{1,0:T(8,128)S(1)} %broadcast_select_fusion.holder_ref, ...), custom_call_target="tpu_custom_call" | custom-call | flops 6442450944 | bytes 33554432 | tf_op jit(solution)/shard_map/update/pallas_call | solution.py:336
  174.0 7.4 %collective-permute-done.22.holder_ref = f32[2048,128]{1,0:T(8,128)S(1)} collective-permute-done((f32[2048,128]{1,0:T(8,128)S(1)}, f32[2048,128]{1,0:T(8,128)S(1)}, u32[]{:S(2)}, u32[]{:S(2)}) %collective-permute-start.22) | collective-permute-done | bytes 1048608 | tf_op jit(solution)/shard_map/ppermute | solution.py:456
  181.4 13.4 %update.3 = f32[2048,4096]{1,0:T(8,128)} custom-call(s32[2]{0:T(128)S(1)} %pad_add_fusion.index_ref, f32[2048,4096]{1,0:T(8,128)} %trailing.7, f32[2048,256]{1,0:T(8,128)S(1)} %pad_maximum_fusion.left_ref, f32[2048,128]{1,0:T(8,128)S(1)} %convolution_add_fusion.1.vectors_ref, ...), custom_call_target="tpu_custom_call", output_to_operand_aliasing={{}: (6, {})} | custom-call | flops 6442450944 | bytes 33554432 | tf_op jit(solution)/shard_map/update/pallas_call | solution.py:336
  (80 shorter events, 43.8 us)
Async XLA Ops:
  1.8 17.5 %collective-permute-start = (f32[1024,128]{1,0:T(8,128)S(1)}, f32[1024,128]{1,0:T(8,128)S(1)}, u32[]{:S(2)}, u32[]{:S(2)}) collective-permute-start(f32[1024,128]{1,0:T(8,128)S(1)} %constant_dynamic-slice_fusion), channel_id=1, source_target_pairs={{0,16},{2,18},{4,20},{6,22},{9,25},{11,27},{13,29},{15,31},{16,0},... | collective-permute-start | bytes 1572872 | tf_op jit(solution)/shard_map/ppermute | solution.py:456
  8.2 4.3 %collective-permute-start.1 = (f32[128,128]{1,0:T(8,128)S(1)}, f32[128,128]{1,0:T(8,128)S(1)}, u32[]{:S(2)}, u32[]{:S(2)}) collective-permute-start(f32[128,128]{1,0:T(8,128)S(1)} %fusion.2), channel_id=1, source_target_pairs={{0,4},{4,0},{8,12},{12,8},{16,20},{20,16},{24,28},{28,24},{1,5},{5... | collective-permute-start | bytes 196616 | tf_op jit(solution)/shard_map/ppermute | solution.py:431
  19.3 11.1 %collective-permute-start.4 = (f32[1024,128]{1,0:T(8,128)S(1)}, f32[1024,128]{1,0:T(8,128)S(1)}, u32[]{:S(2)}, u32[]{:S(2)}) collective-permute-start(f32[1024,128]{1,0:T(8,128)S(1)} %collective-permute-done), channel_id=1, source_target_pairs={{0,2},{4,6},{9,11},{13,15},{18,16},{22,20},{27,25},{31,29}} | collective-permute-start | bytes 1572872 | tf_op jit(solution)/shard_map/ppermute | solution.py:480
  20.6 4.3 %collective-permute-start.2 = (f32[128,128]{1,0:T(8,128)S(1)}, f32[128,128]{1,0:T(8,128)S(1)}, u32[]{:S(2)}, u32[]{:S(2)}) collective-permute-start(f32[128,128]{1,0:T(8,128)S(1)} %add.87), channel_id=1, source_target_pairs={{0,8},{4,12},{8,0},{12,4},{16,24},{20,28},{24,16},{28,20},{1,9},{5... | collective-permute-start | bytes 196616 | tf_op jit(solution)/shard_map/ppermute | solution.py:431
  24.9 5.4 %collective-permute-start.3 = (f32[128,128]{1,0:T(8,128)S(1)}, f32[128,128]{1,0:T(8,128)S(1)}, u32[]{:S(2)}, u32[]{:S(2)}) collective-permute-start(f32[128,128]{1,0:T(8,128)S(1)} %add.88), channel_id=1, source_target_pairs={{0,16},{4,20},{8,24},{12,28},{16,0},{20,4},{24,8},{28,12},{1,17},{... | collective-permute-start | bytes 196616 | tf_op jit(solution)/shard_map/ppermute | solution.py:431
  30.5 14.1 %collective-permute-start.5 = (f32[2048,128]{1,0:T(8,128)S(1)}, f32[2048,128]{1,0:T(8,128)}, u32[]{:S(2)}, u32[]{:S(2)}) collective-permute-start(f32[2048,128]{1,0:T(8,128)S(1)} %maximum_select_fusion.holder_ref), channel_id=1, source_target_pairs={{0,8},{2,10},{4,12},{6,14},{9,1},{11,3},{13,5},{15,7},{16,24},{18,... | collective-permute-start | bytes 3145736 | tf_op jit(solution)/shard_map/ppermute | solution.py:456
  42.1 32.9 %collective-permute-start.6 = (f32[2048,128]{1,0:T(8,128)S(1)}, f32[2048,128]{1,0:T(8,128)}, u32[]{:S(2)}, u32[]{:S(2)}) collective-permute-start(f32[2048,128]{1,0:T(8,128)S(1)} %maximum_select_fusion.holder_ref), channel_id=1, source_target_pairs={{0,4},{2,6},{4,0},{6,2},{9,13},{11,15},{13,9},{15,11},{16,20},{18,... | collective-permute-start | bytes 3145736 | tf_op jit(solution)/shard_map/ppermute | solution.py:456
  44.6 30.4 %collective-permute-start.7 = (f32[2048,128]{1,0:T(8,128)}, f32[2048,128]{1,0:T(8,128)}, u32[]{:S(2)}, u32[]{:S(2)}) collective-permute-start(f32[2048,128]{1,0:T(8,128)} %collective-permute-done.5.other_ref), channel_id=1, source_target_pairs={{1,5},{3,7},{5,1},{7,3},{8,12},{10,14},{12,8},{14,10},{17,21},{19,... | collective-permute-start | bytes 3145736 | tf_op jit(solution)/shard_map/ppermute | solution.py:456
  46.3 5.2 %collective-permute-start.8 = (f32[128,128]{1,0:T(8,128)S(1)}, f32[128,128]{1,0:T(8,128)S(1)}, u32[]{:S(2)}, u32[]{:S(2)}) collective-permute-start(f32[128,128]{1,0:T(8,128)S(1)} %get-tuple-element.36), channel_id=1, source_target_pairs={{0,16},{4,20},{8,24},{12,28},{16,0},{20,4},{24,8},{28,12},{1,17},{... | collective-permute-start | bytes 196616 | tf_op jit(solution)/shard_map/ppermute | solution.py:431
  51.5 5.7 %collective-permute-start.9 = (f32[128,128]{1,0:T(8,128)S(1)}, f32[128,128]{1,0:T(8,128)S(1)}, u32[]{:S(2)}, u32[]{:S(2)}) collective-permute-start(f32[128,128]{1,0:T(8,128)S(1)} %add.90), channel_id=1, source_target_pairs={{0,8},{4,12},{8,0},{12,4},{16,24},{20,28},{24,16},{28,20},{1,9},{5... | collective-permute-start | bytes 196616 | tf_op jit(solution)/shard_map/ppermute | solution.py:431
  57.2 13.8 %collective-permute-start.10 = (f32[128,128]{1,0:T(8,128)S(1)}, f32[128,128]{1,0:T(8,128)S(1)}, u32[]{:S(2)}, u32[]{:S(2)}) collective-permute-start(f32[128,128]{1,0:T(8,128)S(1)} %add.91), channel_id=1, source_target_pairs={{0,4},{4,0},{8,12},{12,8},{16,20},{20,16},{24,28},{28,24},{1,5},{5... | collective-permute-start | bytes 196616 | tf_op jit(solution)/shard_map/ppermute | solution.py:431
  93.5 15.7 %collective-permute-start.12 = (f32[1024,128]{1,0:T(8,128)}, f32[1024,128]{1,0:T(8,128)}, u32[]{:S(2)}, u32[]{:S(2)}) collective-permute-start(f32[1024,128]{1,0:T(8,128)} %add.94), channel_id=1, source_target_pairs={{0,2},{1,3},{2,0},{3,1},{4,6},{5,7},{6,4},{7,5},{8,10},{9,11},{10,... | collective-permute-start | bytes 1572872 | tf_op jit(solution)/shard_map/ppermute | solution.py:431
  95.3 4.3 %collective-permute-start.13 = (f32[128,128]{1,0:T(8,128)S(1)}, f32[128,128]{1,0:T(8,128)S(1)}, u32[]{:S(2)}, u32[]{:S(2)}) collective-permute-start(f32[128,128]{1,0:T(8,128)S(1)} %get-tuple-element.45), channel_id=1, source_target_pairs={{0,4},{4,0},{8,12},{12,8},{16,20},{20,16},{24,28},{28,24},{1,5},{5... | collective-permute-start | bytes 196616 | tf_op jit(solution)/shard_map/ppermute | solution.py:431
  99.6 4.3 %collective-permute-start.14 = (f32[128,128]{1,0:T(8,128)S(1)}, f32[128,128]{1,0:T(8,128)S(1)}, u32[]{:S(2)}, u32[]{:S(2)}) collective-permute-start(f32[128,128]{1,0:T(8,128)S(1)} %add.95), channel_id=1, source_target_pairs={{0,8},{4,12},{8,0},{12,4},{16,24},{20,28},{24,16},{28,20},{1,9},{5... | collective-permute-start | bytes 196616 | tf_op jit(solution)/shard_map/ppermute | solution.py:431
  103.9 5.2 %collective-permute-start.15 = (f32[128,128]{1,0:T(8,128)S(1)}, f32[128,128]{1,0:T(8,128)S(1)}, u32[]{:S(2)}, u32[]{:S(2)}) collective-permute-start(f32[128,128]{1,0:T(8,128)S(1)} %add.96), channel_id=1, source_target_pairs={{0,16},{4,20},{8,24},{12,28},{16,0},{20,4},{24,8},{28,12},{1,17},{... | collective-permute-start | bytes 196616 | tf_op jit(solution)/shard_map/ppermute | solution.py:431
  111.3 2.3 %collective-permute-start.16 = (f32[1024,128]{1,0:T(8,128)}, f32[1024,128]{1,0:T(8,128)}, u32[]{:S(2)}, u32[]{:S(2)}) collective-permute-start(f32[1024,128]{1,0:T(8,128)} %get-tuple-element.52), channel_id=1, source_target_pairs={{0,1},{1,0},{2,3},{3,2},{4,5},{5,4},{6,7},{7,6},{8,9},{9,8},{10,11... | collective-permute-start | bytes 1572872 | tf_op jit(solution)/shard_map/ppermute | solution.py:431
  114.6 29.0 %collective-permute-start.21 = (f32[2048,128]{1,0:T(8,128)S(1)}, f32[2048,128]{1,0:T(8,128)}, u32[]{:S(2)}, u32[]{:S(2)}) collective-permute-start(f32[2048,128]{1,0:T(8,128)S(1)} %constant_dynamic-update-slice_fusion), channel_id=1, source_target_pairs={{0,16},{4,20},{9,25},{13,29},{18,2},{22,6},{27,11},{31,15}} | collective-permute-start | bytes 3145736 | tf_op jit(solution)/shard_map/ppermute | solution.py:456
  117.2 2.2 %collective-permute-start.19 = (f32[128,128]{1,0:T(8,128)S(1)}, f32[128,128]{1,0:T(8,128)S(1)}, u32[]{:S(2)}, u32[]{:S(2)}) collective-permute-start(f32[128,128]{1,0:T(8,128)S(1)} %add.97), channel_id=1, source_target_pairs={{0,1},{1,0},{2,3},{3,2},{4,5},{5,4},{6,7},{7,6},{8,9},{9,8},{10,11... | collective-permute-start | bytes 196616 | tf_op jit(solution)/shard_map/ppermute | solution.py:431
  117.7 6.1 %collective-permute-start.17 = (f32[128,128]{1,0:T(8,128)S(1)}, f32[128,128]{1,0:T(8,128)S(1)}, u32[]{:S(2)}, u32[]{:S(2)}) collective-permute-start(f32[128,128]{1,0:T(8,128)S(1)} %select_add_fusion), channel_id=1, source_target_pairs={{0,1},{4,5},{8,9},{12,13},{16,17},{20,21},{24,25},{28,29}} | collective-permute-start | bytes 196616 | tf_op jit(solution)/shard_map/ppermute | solution.py:507
  119.4 34.2 %collective-permute-start.20 = (f32[128,128]{1,0:T(8,128)S(1)}, f32[128,128]{1,0:T(8,128)S(1)}, u32[]{:S(2)}, u32[]{:S(2)}) collective-permute-start(f32[128,128]{1,0:T(8,128)S(1)} %add.101), channel_id=1, source_target_pairs={{0,2},{1,3},{2,0},{3,1},{4,6},{5,7},{6,4},{7,5},{8,10},{9,11},{10,... | collective-permute-start | bytes 196616 | tf_op jit(solution)/shard_map/ppermute | solution.py:431
  123.8 22.7 %collective-permute-start.18 = (f32[128,128]{1,0:T(8,128)S(1)}, f32[128,128]{1,0:T(8,128)S(1)}, u32[]{:S(2)}, u32[]{:S(2)}) collective-permute-start(f32[128,128]{1,0:T(8,128)S(1)} %broadcast_select_fusion.1), channel_id=1, source_target_pairs={{0,2},{1,3},{4,6},{5,7},{8,10},{9,11},{12,14},{13,15},{16,18},{17,... | collective-permute-start | bytes 196616 | tf_op jit(solution)/shard_map/ppermute | solution.py:507
  145.0 13.6 %collective-permute-start.23 = (f32[2048,128]{1,0:T(8,128)S(1)}, f32[2048,128]{1,0:T(8,128)S(1)}, u32[]{:S(2)}, u32[]{:S(2)}) collective-permute-start(f32[2048,128]{1,0:T(8,128)S(1)} %broadcast_select_fusion.holder_ref), channel_id=1, source_target_pairs={{0,8},{2,10},{4,12},{6,14},{9,1},{11,3},{13,5},{15,7},{16,24},{18,... | collective-permute-start | bytes 3145736 | tf_op jit(solution)/shard_map/ppermute | solution.py:456
  156.1 25.4 %collective-permute-start.22 = (f32[2048,128]{1,0:T(8,128)S(1)}, f32[2048,128]{1,0:T(8,128)S(1)}, u32[]{:S(2)}, u32[]{:S(2)}) collective-permute-start(f32[2048,128]{1,0:T(8,128)S(1)} %broadcast_select_fusion.holder_ref), channel_id=1, source_target_pairs={{0,4},{2,6},{4,0},{6,2},{9,13},{11,15},{13,9},{15,11},{16,20},{18,... | collective-permute-start | bytes 3145736 | tf_op jit(solution)/shard_map/ppermute | solution.py:456
  158.6 22.9 %collective-permute-start.24 = (f32[2048,128]{1,0:T(8,128)S(1)}, f32[2048,128]{1,0:T(8,128)S(1)}, u32[]{:S(2)}, u32[]{:S(2)}) collective-permute-start(f32[2048,128]{1,0:T(8,128)S(1)} %collective-permute-done.23.other_ref), channel_id=1, source_target_pairs={{1,5},{3,7},{5,1},{7,3},{8,12},{10,14},{12,8},{14,10},{17,21},{19,... | collective-permute-start | bytes 3145736 | tf_op jit(solution)/shard_map/ppermute | solution.py:456
  (7 other events, 50.1 us)
where the time goes:
time: 196 us; the launch traced here: 195 us
  waiting for transfers between devices  70.3 us (36%)
  Pallas kernels  68.4 us (35%)
  starting transfers between devices  38.4 us (20%)
  matrix products  7.24 us (4%)
  other arithmetic  5.02 us (3%)
  local copies, waits for them, and re-layouts  4.47 us (2%)
    ppermute x14, waiting for transfers between devices, swap(): return lax.ppermute(value, axis, [(i, i ^ bit) for i in range(count)])  37.4 us
    ppermute x8, waiting for transfers between devices, move(): return lax.ppermute(value, ('row', 'col'), pairs)  32.8 us
    pallas_call x2, Pallas kernels, update(): pl.pallas_call(update_kernel, out_shape=jax.ShapeDtypeStruct(trailing.sha...  26.8 us
    pallas_call x2, Pallas kernels, product(): pl.pallas_call(product_kernel, out_shape=(jax.ShapeDtypeStruct((rows, wid...  18.9 us
    ppermute x14, starting transfers between devices, swap(): return lax.ppermute(value, axis, [(i, i ^ bit) for i in range(count)])  17.9 us
    ppermute x8, starting transfers between devices, move(): return lax.ppermute(value, ('row', 'col'), pairs)  17.3 us
    pallas_call x1, Pallas kernels, first_pass(): pl.pallas_call(first_kernel, out_shape=(square, square, jax.ShapeDtypeStr...  7.94 us
    pallas_call x1, Pallas kernels, small_pass(): pl.pallas_call(small_kernel, out_shape=(square, square), compiler_params=...  7 us
  transfers between devices with their start and end apart: 25, of which 15 were waited for; matrix products, arithmetic and copies ran while one was open for 5% of the time, Pallas kernels for 21%

commit v1 on v0

--- a/solution.py
+++ b/solution.py
@@ -180,15 +180,13 @@
 def fetch(away, holder, other, into, sem):
     @pl.when(away == 0)
     def _():
-        copy = pltpu.make_async_copy(holder, into, sem)
-        copy.start()
-        copy.wait()
+        pltpu.make_async_copy(holder, into, sem).start()
 
     @pl.when(away != 0)
     def _():
-        copy = pltpu.make_async_copy(other, into, sem)
-        copy.start()
-        copy.wait()
+        pltpu.make_async_copy(other, into, sem).start()
+
+    return pltpu.make_async_copy(holder, into, sem)
 
 
 def chunk_of(rows):
@@ -209,10 +207,11 @@
         slot = i % slots
         return pltpu.make_async_copy(trailing.at[part, columns], tiles.at[slot], sems.at[slot])
 
+    fetched = fetch(index_ref[1], holder_ref, other_ref, panel, sem)
     for i in range(slots):
         load(i).start()
 
-    fetch(index_ref[1], holder_ref, other_ref, panel, sem)
+    fetched.wait()
     basis_ref[...] = dot_nt(panel[...], inverse_ref[...])
     high, low = split(basis_ref[...])
     both[:, :width] = high
@@ -261,7 +260,7 @@
             pltpu.SemaphoreType.DMA,
             pltpu.SemaphoreType.DMA((slots,)),
         ],
-        compiler_params=pltpu.CompilerParams(vmem_limit_bytes=20 * 1024 * 1024),
+        compiler_params=pltpu.CompilerParams(vmem_limit_bytes=28 * 1024 * 1024),
         cost_estimate=pl.CostEstimate(
             flops=8 * rows * depth * width, bytes_accessed=4 * rows * depth, transcendentals=0
         ),
@@ -289,10 +288,11 @@
         slot = i % slots
         return pltpu.make_async_copy(tiles.at[slot], out.at[part, columns], stores.at[slot])
 
+    fetched = fetch(index_ref[1], holder_ref, other_ref, applied, sem)
     for i in range(min(ahead, count)):
         load(i).start()
 
-    fetch(index_ref[1], holder_ref, other_ref, applied, sem)
+    fetched.wait()
     for place, ref in ((0, applied), (width, vectors_ref)):
         high, low = split(ref[...].T)
         right[place : place + width, :] = high
@@ -355,7 +355,7 @@
             pltpu.SemaphoreType.DMA((slots,)),
         ],
         input_output_aliases=aliases,
-        compiler_params=pltpu.CompilerParams(vmem_limit_bytes=26 * 1024 * 1024),
+        compiler_params=pltpu.CompilerParams(vmem_limit_bytes=30 * 1024 * 1024),
         cost_estimate=pl.CostEstimate(
             flops=12 * rows * depth * width, bytes_accessed=8 * rows * depth, transcendentals=0
         ),
@@ -417,7 +417,7 @@
             in_specs=[piece, piece, square, piece],
             out_specs=(whole, whole, piece, square),
         ),
-        compiler_params=pltpu.CompilerParams(vmem_limit_bytes=24 * 1024 * 1024),
+        compiler_params=pltpu.CompilerParams(vmem_limit_bytes=30 * 1024 * 1024),
         name="applied",
     )(index, raw, basis, inverse, trailing)
 
@@ -466,11 +466,11 @@
             done |= bit
         return value
 
-    def relay_halves(self, value, meanwhile):
+    def second_half(self):
+        return (self.away == self.col_n // 2).astype(jnp.int32)
+
+    def relay_halves(self, value, piece, meanwhile):
         bit = self.col_n // 2
-        half = value.shape[0] // 2
-        across = (self.away == bit).astype(jnp.int32)
-        piece = lax.dynamic_slice_in_dim(value, across * half, half, 0)
         first = self.move(piece, lambda d: d & ~bit == 0, lambda r: r ^ (bit * self.ratio))
         first, meanwhile = lax.optimization_barrier((first, meanwhile))
         pairs = []
@@ -479,7 +479,7 @@
             pairs.append((r * self.col_n + c, r * self.col_n + (c ^ bit)))
         second = lax.ppermute(first, ("row", "col"), pairs)
         moved = jnp.concatenate([first, second])
-        return jnp.where(self.away == bit, moved, value), meanwhile
+        return self.relay(jnp.where(self.away == bit, moved, value), bit), meanwhile
 
     def near(self, value):
         holds = lambda d: d & 1 == 0
@@ -526,19 +526,20 @@
         return jnp.stack([part ^ low, gather.away & 1]).astype(jnp.int32)
 
     gram = sum_small(dot_tn(panel_block, panel_block), "row", row_bits[:1])
-    relayed, gram = gather.relay_halves(panel_block, gram)
-    relayed = gather.relay(relayed, lax.axis_size("col") // 2)
+    piece = lax.dynamic_slice_in_dim(panel_block, gather.second_half() * half, half, 0)
+    relayed, gram = gather.relay_halves(panel_block, piece, gram)
     gram = sum_small(gram, "row", row_bits[1:])
     moved_high, moved_low = gather.near(after(relayed, gram))
     first_factor, first_inverse, first_basis, second = first_pass(gram, panel_block)
 
+    second = sum_small(second, "row", row_bits[:1])
     moved_high, second = lax.optimization_barrier((moved_high, second))
     parts = [(relayed, moved_high), (moved_low, gather.across(moved_high))]
     raw, basis = product(
         index_of(0), trailing, first_inverse, jnp.zeros((shard_rows, width), F32), *parts[0]
     )
     bases = [basis]
-    second = sum_small(second, "row", row_bits[::-1])
+    second = sum_small(second, "row", row_bits[:0:-1])
     parts += gather.rest(parts)
     for part in range(1, ratio):
         raw, basis = product(index_of(part), trailing, first_inverse, raw, *parts[part])
@@ -558,16 +559,18 @@
     for bit in col_bits[1:]:
         moved, inner = lax.optimization_barrier((swap(keep, "col", bit), inner))
         keep = keep + moved
+    keep = lax.optimization_barrier(keep)
     other = swap(keep, "col", col_bits[0])
     applied = jnp.zeros((shard_rows, width), F32)
     applied = lax.dynamic_update_slice_in_dim(applied, keep, mine * half, 0)
     applied = lax.dynamic_update_slice_in_dim(applied, other, (1 - mine) * half, 0)
 
-    relayed = gather.relay(applied)
-    inner = sum_small(inner, "col", col_bits)
+    piece = jnp.where(mine == gather.second_half(), keep, other)
     top = sum(jnp.where(low == part, basis[:width], 0.0) for part, basis in enumerate(bases))
-    top = broadcast_col(after(top, applied))
+    top = broadcast_col(after(top, piece))
     band_block, kernel = small_pass(second_upper, second_inverse, first_factor, top)
+    inner = sum_small(after(inner, piece), "col", col_bits)
+    relayed, (inner, kernel) = gather.relay_halves(applied, piece, (inner, kernel))
     inner = dot_tn(kernel, dot_nn(inner, kernel))
     left = jnp.concatenate(
         [dot_nt(vectors, kernel), dot_nn(applied, kernel) - dot_nn(vectors, inner)], axis=1
@@ -576,6 +579,7 @@
         dot_nt(basis, second_inverse) + identity_rows((col * ratio + (part ^ low)) * shard_rows)
         for part, basis in enumerate(bases)
     ]
+    relayed, left, *block_vectors = lax.optimization_barrier((relayed, left, *block_vectors))
     moved_high, moved_low = gather.near(relayed)
     parts = [(relayed, moved_high), (moved_low, gather.across(moved_high))]
     reduced = update(index_of(0), trailing, left, block_vectors[0], *parts[0], None)

time: 196 us -> 183 us (0.934)
  the two profiles are of different devices: /device:TPU:6 before, /device:TPU:12 now
where the time goes in v1:
time: 183 us; the launch traced here: 182 us
  Pallas kernels  68.1 us (37%)
  waiting for transfers between devices  55.7 us (30%)
  starting transfers between devices  42.7 us (23%)
  matrix products  7.23 us (4%)
  other arithmetic  3.89 us (2%)
  local copies, waits for them, and re-layouts  3.24 us (2%)
    ppermute x14, waiting for transfers between devices, swap(): return lax.ppermute(value, axis, [(i, i ^ bit) for i in range(count)])  33.3 us
    pallas_call x2, Pallas kernels, update(): pl.pallas_call(update_kernel, out_shape=jax.ShapeDtypeStruct(trailing.sha...  26.9 us
    ppermute x14, starting transfers between devices, swap(): return lax.ppermute(value, axis, [(i, i ^ bit) for i in range(count)])  26 us
    ppermute x8, waiting for transfers between devices, move(): return lax.ppermute(value, ('row', 'col'), pairs)  21.1 us
    pallas_call x2, Pallas kernels, product(): pl.pallas_call(product_kernel, out_shape=(jax.ShapeDtypeStruct((rows, wid...  18.6 us
    ppermute x8, starting transfers between devices, move(): return lax.ppermute(value, ('row', 'col'), pairs)  13 us
    pallas_call x1, Pallas kernels, first_pass(): pl.pallas_call(first_kernel, out_shape=(square, square, jax.ShapeDtypeStr...  7.94 us
    pallas_call x1, Pallas kernels, small_pass(): pl.pallas_call(small_kernel, out_shape=(square, square), compiler_params=...  7.01 us
  transfers between devices with their start and end apart: 26, of which 13 were waited for; matrix products, arithmetic and copies ran while one was open for 5% of the time, Pallas kernels for 22%

profile of v1, /device:TPU:12, one launch (start us, length us, event | category | flops | bytes accessed | tf_op | source)
XLA Modules:
  0.0 182.3 jit_solution(15965445466925113606)
XLA Ops:
  5.9 2.8 %collective-permute-done.1 = f32[128,128]{1,0:T(8,128)S(1)} collective-permute-done((f32[128,128]{1,0:T(8,128)S(1)}, f32[128,128]{1,0:T(8,128)S(1)}, u32[]{:S(2)}, u32[]{:S(2)}) %collective-permute-start.1) | collective-permute-done | bytes 65568 | tf_op jit(solution)/shard_map/ppermute | solution.py:431
  9.4 11.7 %collective-permute-start.2 = (f32[128,128]{1,0:T(8,128)S(1)}, f32[128,128]{1,0:T(8,128)S(1)}, u32[]{:S(2)}, u32[]{:S(2)}) collective-permute-start(f32[128,128]{1,0:T(8,128)S(1)} %add.87), channel_id=1, source_target_pairs={{0,8},{4,12},{8,0},{12,4},{16,24},{20,28},{24,16},{28,20},{1,9},{5... | collective-permute-start | bytes 196616 | tf_op jit(solution)/shard_map/ppermute | solution.py:431
  21.1 2.2 %collective-permute-done.2 = f32[128,128]{1,0:T(8,128)S(1)} collective-permute-done((f32[128,128]{1,0:T(8,128)S(1)}, f32[128,128]{1,0:T(8,128)S(1)}, u32[]{:S(2)}, u32[]{:S(2)}) %collective-permute-start.2) | collective-permute-done | bytes 65568 | tf_op jit(solution)/shard_map/ppermute | solution.py:431
  23.9 4.7 %collective-permute-done.3 = f32[128,128]{1,0:T(8,128)S(1)} collective-permute-done((f32[128,128]{1,0:T(8,128)S(1)}, f32[128,128]{1,0:T(8,128)S(1)}, u32[]{:S(2)}, u32[]{:S(2)}) %collective-permute-start.3) | collective-permute-done | bytes 65568 | tf_op jit(solution)/shard_map/ppermute | solution.py:431
  30.0 7.9 %first_pass.1 = (f32[128,128]{1,0:T(8,128)}, f32[128,128]{1,0:T(8,128)S(1)}, f32[2048,128]{1,0:T(8,128)S(1)}, f32[128,128]{1,0:T(8,128)S(1)}) custom-call(f32[128,128]{1,0:T(8,128)S(1)} %add.89.gram_ref, f32[2048,128]{1,0:T(8,128)S(1)} %copy-done), custom_call_target="tpu_custom_call" | custom-call | tf_op jit(solution)/shard_map/first_pass/pallas_call | solution.py:131
  40.4 2.8 %collective-permute-done.6 = f32[128,128]{1,0:T(8,128)S(1)} collective-permute-done((f32[128,128]{1,0:T(8,128)S(1)}, f32[128,128]{1,0:T(8,128)S(1)}, u32[]{:S(2)}, u32[]{:S(2)}) %collective-permute-start.6) | collective-permute-done | bytes 65568 | tf_op jit(solution)/shard_map/ppermute | solution.py:431
  45.4 3.4 %collective-permute-start.8 = (f32[2048,128]{1,0:T(8,128)S(1)}, f32[2048,128]{1,0:T(8,128)}, u32[]{:S(2)}, u32[]{:S(2)}) collective-permute-start(f32[2048,128]{1,0:T(8,128)S(1)} %collective-permute-done.5.other_ref), channel_id=1, source_target_pairs={{1,5},{3,7},{5,1},{7,3},{8,12},{10,14},{12,8},{14,10},{17,21},{19,... | collective-permute-start | bytes 3145736 | tf_op jit(solution)/shard_map/ppermute | solution.py:456
  49.8 4.4 %collective-permute-done.9 = f32[128,128]{1,0:T(8,128)S(1)} collective-permute-done((f32[128,128]{1,0:T(8,128)S(1)}, f32[128,128]{1,0:T(8,128)S(1)}, u32[]{:S(2)}, u32[]{:S(2)}) %collective-permute-start.9) | collective-permute-done | bytes 65568 | tf_op jit(solution)/shard_map/ppermute | solution.py:431
  54.2 2.2 %collective-permute-start.10 = (f32[128,128]{1,0:T(8,128)S(1)}, f32[128,128]{1,0:T(8,128)S(1)}, u32[]{:S(2)}, u32[]{:S(2)}) collective-permute-start(f32[128,128]{1,0:T(8,128)S(1)} %add.91), channel_id=1, source_target_pairs={{0,8},{4,12},{8,0},{12,4},{16,24},{20,28},{24,16},{28,20},{1,9},{5... | collective-permute-start | bytes 196616 | tf_op jit(solution)/shard_map/ppermute | solution.py:431
  56.5 8.2 %product.2 = (f32[2048,128]{1,0:T(8,128)S(1)}, f32[2048,128]{1,0:T(8,128)S(1)}) custom-call(s32[2]{0:T(128)S(1)} %pad_add_fusion.2.index_ref._, f32[2048,4096]{1,0:T(8,128)} %trailing.7, f32[128,128]{1,0:T(8,128)S(1)} %get-tuple-element.36.inverse_ref, f32[2048,128]{1,0:T(8,128)S(1)} %broadcast_1_before_ref.2.before_ref, ...), custom_call_target="tpu_custom_call" | custom-call | flops 4294967296 | bytes 16777216 | tf_op jit(solution)/shard_map/product/pallas_call | solution.py:241
  65.7 4.1 %second_pass.1 = (f32[128,128]{1,0:T(8,128)S(1)}, f32[128,128]{1,0:T(8,128)S(1)}) custom-call(f32[128,128]{1,0:T(8,128)S(1)} %add.92.gram_ref), custom_call_target="tpu_custom_call" | custom-call | tf_op jit(solution)/shard_map/second_pass/pallas_call | solution.py:147
  69.7 10.4 %product.3 = (f32[2048,128]{1,0:T(8,128)S(1)}, f32[2048,128]{1,0:T(8,128)S(1)}) custom-call(s32[2]{0:T(128)S(1)} %pad_add_fusion.index_ref, f32[2048,4096]{1,0:T(8,128)} %trailing.7, f32[128,128]{1,0:T(8,128)S(1)} %get-tuple-element.36.inverse_ref, f32[2048,128]{1,0:T(8,128)S(1)} %get-tuple-element.41.before_ref, ...), custom_call_target="tpu_custom_call" | custom-call | flops 4294967296 | bytes 16777216 | tf_op jit(solution)/shard_map/product/pallas_call | solution.py:241
  80.2 3.6 %applied.1 = (f32[1024,128]{1,0:T(8,128)S(1)}, f32[1024,128]{1,0:T(8,128)S(1)}, f32[2048,128]{1,0:T(8,128)S(1)}, f32[128,128]{1,0:T(8,128)S(1)}) custom-call(s32[3]{0:T(128)S(1)} %pad_add_fusion.1.index_ref, f32[2048,128]{1,0:T(8,128)S(1)} %get-tuple-element.42.raw_ref, f32[2048,128]{1,0:T(8,128)S(1)} %copy-done.4, ...), custom_call_target="tpu_custom_call" | custom-call | tf_op jit(solution)/shard_map/applied/pallas_call | solution.py:406
  83.9 1.9 %collective-permute-done.11 = f32[1024,128]{1,0:T(8,128)S(1)} collective-permute-done((f32[1024,128]{1,0:T(8,128)S(1)}, f32[1024,128]{1,0:T(8,128)S(1)}, u32[]{:S(2)}, u32[]{:S(2)}) %collective-permute-start.11) | collective-permute-done | bytes 524320 | tf_op jit(solution)/shard_map/ppermute | solution.py:431
  86.7 2.7 %collective-permute-start.12 = (f32[1024,128]{1,0:T(8,128)}, f32[1024,128]{1,0:T(8,128)}, u32[]{:S(2)}, u32[]{:S(2)}) collective-permute-start(f32[1024,128]{1,0:T(8,128)} %add.93), channel_id=1, source_target_pairs={{0,2},{1,3},{2,0},{3,1},{4,6},{5,7},{6,4},{7,5},{8,10},{9,11},{10,... | collective-permute-start | bytes 1572872 | tf_op jit(solution)/shard_map/ppermute | solution.py:431
  89.8 3.8 %collective-permute-done.13 = f32[128,128]{1,0:T(8,128)S(1)} collective-permute-done((f32[128,128]{1,0:T(8,128)S(1)}, f32[128,128]{1,0:T(8,128)S(1)}, u32[]{:S(2)}, u32[]{:S(2)}) %collective-permute-start.13) | collective-permute-done | bytes 65568 | tf_op jit(solution)/shard_map/ppermute | solution.py:431
  93.7 4.6 %collective-permute-done.14 = f32[128,128]{1,0:T(8,128)S(1)} collective-permute-done((f32[128,128]{1,0:T(8,128)S(1)}, f32[128,128]{1,0:T(8,128)S(1)}, u32[]{:S(2)}, u32[]{:S(2)}) %collective-permute-start.14) | collective-permute-done | bytes 65568 | tf_op jit(solution)/shard_map/ppermute | solution.py:431
  98.5 5.1 %collective-permute-done.15 = f32[128,128]{1,0:T(8,128)S(1)} collective-permute-done((f32[128,128]{1,0:T(8,128)S(1)}, f32[128,128]{1,0:T(8,128)S(1)}, u32[]{:S(2)}, u32[]{:S(2)}) %collective-permute-start.15) | collective-permute-done | bytes 65568 | tf_op jit(solution)/shard_map/ppermute | solution.py:431
  113.7 2.7 %collective-permute-start.19 = (f32[128,128]{1,0:T(8,128)S(1)}, f32[128,128]{1,0:T(8,128)S(1)}, u32[]{:S(2)}, u32[]{:S(2)}) collective-permute-start(f32[128,128]{1,0:T(8,128)S(1)} %add.98), channel_id=1, source_target_pairs={{0,2},{1,3},{2,0},{3,1},{4,6},{5,7},{6,4},{7,5},{8,10},{9,11},{10,... | collective-permute-start | bytes 196616 | tf_op jit(solution)/shard_map/ppermute | solution.py:431
  117.7 7.0 %small_pass.1 = (f32[128,128]{1,0:T(8,128)}, f32[128,128]{1,0:T(8,128)S(1)}) custom-call(f32[128,128]{1,0:T(8,128)S(1)} %get-tuple-element.52.upper_ref, f32[128,128]{1,0:T(8,128)S(1)} %get-tuple-element.45.inverse_ref, f32[128,128]{1,0:T(8,128)S(1)} %copy-done.5, f32[128,128]{1,0:T(8,128)S(1)} %broadcast_select_fusion.2.top_ref), custom_call_target="tpu_custom_call" | custom-call | tf_op jit(solution)/shard_map/small_pass/pallas_call | solution.py:167
  131.3 20.5 %collective-permute-done.24.other_ref = f32[2048,128]{1,0:T(8,128)S(1)} collective-permute-done((f32[2048,128]{1,0:T(8,128)S(1)}, f32[2048,128]{1,0:T(8,128)S(1)}, u32[]{:S(2)}, u32[]{:S(2)}) %collective-permute-start.24) | collective-permute-done | bytes 1048608 | tf_op jit(solution)/shard_map/ppermute | solution.py:456
  151.8 3.3 %collective-permute-start.25 = (f32[2048,128]{1,0:T(8,128)S(1)}, f32[2048,128]{1,0:T(8,128)S(1)}, u32[]{:S(2)}, u32[]{:S(2)}) collective-permute-start(f32[2048,128]{1,0:T(8,128)S(1)} %collective-permute-done.24.other_ref), channel_id=1, source_target_pairs={{1,5},{3,7},{5,1},{7,3},{8,12},{10,14},{12,8},{14,10},{17,21},{19,... | collective-permute-start | bytes 3145736 | tf_op jit(solution)/shard_map/ppermute | solution.py:456
  155.1 13.5 %update.2._ = f32[2048,4096]{1,0:T(8,128)} custom-call(s32[2]{0:T(128)S(1)} %pad_add_fusion.2.index_ref._, f32[2048,4096]{1,0:T(8,128)} %trailing.7, f32[2048,256]{1,0:T(8,128)S(1)} %pad_maximum_fusion.left_ref, f32[2048,128]{1,0:T(8,128)S(1)} %convolution_add_fusion.1.vectors_ref, f32[2048,128]{1,0:T(8,128)S(1)} %maximum_select_fusion.1.holder_ref, ...), custom_call_target="tpu_custom_call" | custom-call | flops 6442450944 | bytes 33554432 | tf_op jit(solution)/shard_map/update/pallas_call | solution.py:336
  168.6 13.5 %update.3 = f32[2048,4096]{1,0:T(8,128)} custom-call(s32[2]{0:T(128)S(1)} %pad_add_fusion.index_ref, f32[2048,4096]{1,0:T(8,128)} %trailing.7, f32[2048,256]{1,0:T(8,128)S(1)} %pad_maximum_fusion.left_ref, f32[2048,128]{1,0:T(8,128)S(1)} %convolution_add_fusion.vectors_ref, ...), custom_call_target="tpu_custom_call", output_to_operand_aliasing={{}: (6, {})} | custom-call | flops 6442450944 | bytes 33554432 | tf_op jit(solution)/shard_map/update/pallas_call | solution.py:336
  (84 shorter events, 34.0 us)
Async XLA Ops:
  1.8 6.9 %collective-permute-start = (f32[1024,128]{1,0:T(8,128)S(1)}, f32[1024,128]{1,0:T(8,128)S(1)}, u32[]{:S(2)}, u32[]{:S(2)}) collective-permute-start(f32[1024,128]{1,0:T(8,128)S(1)} %constant_dynamic-slice_fusion), channel_id=1, source_target_pairs={{0,16},{2,18},{4,20},{6,22},{9,25},{11,27},{13,29},{15,31},{16,0},... | collective-permute-start | bytes 1572872 | tf_op jit(solution)/shard_map/ppermute | solution.py:456
  4.4 4.3 %collective-permute-start.1 = (f32[128,128]{1,0:T(8,128)S(1)}, f32[128,128]{1,0:T(8,128)S(1)}, u32[]{:S(2)}, u32[]{:S(2)}) collective-permute-start(f32[128,128]{1,0:T(8,128)S(1)} %fusion), channel_id=1, source_target_pairs={{0,4},{4,0},{8,12},{12,8},{16,20},{20,16},{24,28},{28,24},{1,5},{5... | collective-permute-start | bytes 196616 | tf_op jit(solution)/shard_map/ppermute | solution.py:431
  8.7 19.9 %collective-permute-start.4 = (f32[1024,128]{1,0:T(8,128)S(1)}, f32[1024,128]{1,0:T(8,128)S(1)}, u32[]{:S(2)}, u32[]{:S(2)}) collective-permute-start(f32[1024,128]{1,0:T(8,128)S(1)} %collective-permute-done), channel_id=1, source_target_pairs={{0,2},{4,6},{9,11},{13,15},{18,16},{22,20},{27,25},{31,29}} | collective-permute-start | bytes 1572872 | tf_op jit(solution)/shard_map/ppermute | solution.py:480
  9.4 13.9 %collective-permute-start.2 = (f32[128,128]{1,0:T(8,128)S(1)}, f32[128,128]{1,0:T(8,128)S(1)}, u32[]{:S(2)}, u32[]{:S(2)}) collective-permute-start(f32[128,128]{1,0:T(8,128)S(1)} %add.87), channel_id=1, source_target_pairs={{0,8},{4,12},{8,0},{12,4},{16,24},{20,28},{24,16},{28,20},{1,9},{5... | collective-permute-start | bytes 196616 | tf_op jit(solution)/shard_map/ppermute | solution.py:431
  23.4 5.2 %collective-permute-start.3 = (f32[128,128]{1,0:T(8,128)S(1)}, f32[128,128]{1,0:T(8,128)S(1)}, u32[]{:S(2)}, u32[]{:S(2)}) collective-permute-start(f32[128,128]{1,0:T(8,128)S(1)} %add.88), channel_id=1, source_target_pairs={{0,16},{4,20},{8,24},{12,28},{16,0},{20,4},{24,8},{28,12},{1,17},{... | collective-permute-start | bytes 196616 | tf_op jit(solution)/shard_map/ppermute | solution.py:431
  28.7 16.7 %collective-permute-start.5 = (f32[2048,128]{1,0:T(8,128)S(1)}, f32[2048,128]{1,0:T(8,128)S(1)}, u32[]{:S(2)}, u32[]{:S(2)}) collective-permute-start(f32[2048,128]{1,0:T(8,128)S(1)} %maximum_select_fusion.holder_ref), channel_id=1, source_target_pairs={{0,8},{2,10},{4,12},{6,14},{9,1},{11,3},{13,5},{15,7},{16,24},{18,... | collective-permute-start | bytes 3145736 | tf_op jit(solution)/shard_map/ppermute | solution.py:456
  39.0 4.3 %collective-permute-start.6 = (f32[128,128]{1,0:T(8,128)S(1)}, f32[128,128]{1,0:T(8,128)S(1)}, u32[]{:S(2)}, u32[]{:S(2)}) collective-permute-start(f32[128,128]{1,0:T(8,128)S(1)} %get-tuple-element.39), channel_id=1, source_target_pairs={{0,4},{4,0},{8,12},{12,8},{16,20},{20,16},{24,28},{28,24},{1,5},{5... | collective-permute-start | bytes 196616 | tf_op jit(solution)/shard_map/ppermute | solution.py:431
  43.2 26.5 %collective-permute-start.7 = (f32[2048,128]{1,0:T(8,128)S(1)}, f32[2048,128]{1,0:T(8,128)}, u32[]{:S(2)}, u32[]{:S(2)}) collective-permute-start(f32[2048,128]{1,0:T(8,128)S(1)} %maximum_select_fusion.holder_ref), channel_id=1, source_target_pairs={{0,4},{2,6},{4,0},{6,2},{9,13},{11,15},{13,9},{15,11},{16,20},{18,... | collective-permute-start | bytes 3145736 | tf_op jit(solution)/shard_map/ppermute | solution.py:456
  45.4 24.3 %collective-permute-start.8 = (f32[2048,128]{1,0:T(8,128)S(1)}, f32[2048,128]{1,0:T(8,128)}, u32[]{:S(2)}, u32[]{:S(2)}) collective-permute-start(f32[2048,128]{1,0:T(8,128)S(1)} %collective-permute-done.5.other_ref), channel_id=1, source_target_pairs={{1,5},{3,7},{5,1},{7,3},{8,12},{10,14},{12,8},{14,10},{17,21},{19,... | collective-permute-start | bytes 3145736 | tf_op jit(solution)/shard_map/ppermute | solution.py:456
  49.0 5.2 %collective-permute-start.9 = (f32[128,128]{1,0:T(8,128)S(1)}, f32[128,128]{1,0:T(8,128)S(1)}, u32[]{:S(2)}, u32[]{:S(2)}) collective-permute-start(f32[128,128]{1,0:T(8,128)S(1)} %add.90), channel_id=1, source_target_pairs={{0,16},{4,20},{8,24},{12,28},{16,0},{20,4},{24,8},{28,12},{1,17},{... | collective-permute-start | bytes 196616 | tf_op jit(solution)/shard_map/ppermute | solution.py:431
  54.2 11.5 %collective-permute-start.10 = (f32[128,128]{1,0:T(8,128)S(1)}, f32[128,128]{1,0:T(8,128)S(1)}, u32[]{:S(2)}, u32[]{:S(2)}) collective-permute-start(f32[128,128]{1,0:T(8,128)S(1)} %add.91), channel_id=1, source_target_pairs={{0,8},{4,12},{8,0},{12,4},{16,24},{20,28},{24,16},{28,20},{1,9},{5... | collective-permute-start | bytes 196616 | tf_op jit(solution)/shard_map/ppermute | solution.py:431
  86.7 16.9 %collective-permute-start.12 = (f32[1024,128]{1,0:T(8,128)}, f32[1024,128]{1,0:T(8,128)}, u32[]{:S(2)}, u32[]{:S(2)}) collective-permute-start(f32[1024,128]{1,0:T(8,128)} %add.93), channel_id=1, source_target_pairs={{0,2},{1,3},{2,0},{3,1},{4,6},{5,7},{6,4},{7,5},{8,10},{9,11},{10,... | collective-permute-start | bytes 1572872 | tf_op jit(solution)/shard_map/ppermute | solution.py:431
  89.3 4.3 %collective-permute-start.13 = (f32[128,128]{1,0:T(8,128)S(1)}, f32[128,128]{1,0:T(8,128)S(1)}, u32[]{:S(2)}, u32[]{:S(2)}) collective-permute-start(f32[128,128]{1,0:T(8,128)S(1)} %get-tuple-element.48), channel_id=1, source_target_pairs={{0,4},{4,0},{8,12},{12,8},{16,20},{20,16},{24,28},{28,24},{1,5},{5... | collective-permute-start | bytes 196616 | tf_op jit(solution)/shard_map/ppermute | solution.py:431
  93.6 4.7 %collective-permute-start.14 = (f32[128,128]{1,0:T(8,128)S(1)}, f32[128,128]{1,0:T(8,128)S(1)}, u32[]{:S(2)}, u32[]{:S(2)}) collective-permute-start(f32[128,128]{1,0:T(8,128)S(1)} %add.94), channel_id=1, source_target_pairs={{0,8},{4,12},{8,0},{12,4},{16,24},{20,28},{24,16},{28,20},{1,9},{5... | collective-permute-start | bytes 196616 | tf_op jit(solution)/shard_map/ppermute | solution.py:431
  98.3 5.2 %collective-permute-start.15 = (f32[128,128]{1,0:T(8,128)S(1)}, f32[128,128]{1,0:T(8,128)S(1)}, u32[]{:S(2)}, u32[]{:S(2)}) collective-permute-start(f32[128,128]{1,0:T(8,128)S(1)} %add.95), channel_id=1, source_target_pairs={{0,16},{4,20},{8,24},{12,28},{16,0},{20,4},{24,8},{28,12},{1,17},{... | collective-permute-start | bytes 196616 | tf_op jit(solution)/shard_map/ppermute | solution.py:431
  107.0 4.2 %collective-permute-start.20 = (f32[128,128]{1,0:T(8,128)S(1)}, f32[128,128]{1,0:T(8,128)S(1)}, u32[]{:S(2)}, u32[]{:S(2)}) collective-permute-start(f32[128,128]{1,0:T(8,128)S(1)} %select_add_fusion), channel_id=1, source_target_pairs={{0,1},{4,5},{8,9},{12,13},{16,17},{20,21},{24,25},{28,29}} | collective-permute-start | bytes 196616 | tf_op jit(solution)/shard_map/ppermute | solution.py:507
  108.8 15.9 %collective-permute-start.17 = (f32[1024,128]{1,0:T(8,128)S(1)}, f32[1024,128]{1,0:T(8,128)S(1)}, u32[]{:S(2)}, u32[]{:S(2)}) collective-permute-start(f32[1024,128]{1,0:T(8,128)S(1)} %get-tuple-element.67), channel_id=1, source_target_pairs={{0,16},{2,18},{4,20},{6,22},{9,25},{11,27},{13,29},{15,31},{16,0},... | collective-permute-start | bytes 1572872 | tf_op jit(solution)/shard_map/ppermute | solution.py:456
  109.5 4.2 %collective-permute-start.18 = (f32[128,128]{1,0:T(8,128)S(1)}, f32[128,128]{1,0:T(8,128)S(1)}, u32[]{:S(2)}, u32[]{:S(2)}) collective-permute-start(f32[128,128]{1,0:T(8,128)S(1)} %add.96), channel_id=1, source_target_pairs={{0,1},{1,0},{2,3},{3,2},{4,5},{5,4},{6,7},{7,6},{8,9},{9,8},{10,11... | collective-permute-start | bytes 196616 | tf_op jit(solution)/shard_map/ppermute | solution.py:431
  111.2 6.5 %collective-permute-start.21 = (f32[128,128]{1,0:T(8,128)S(1)}, f32[128,128]{1,0:T(8,128)S(1)}, u32[]{:S(2)}, u32[]{:S(2)}) collective-permute-start(f32[128,128]{1,0:T(8,128)S(1)} %broadcast_select_fusion.1), channel_id=1, source_target_pairs={{0,2},{1,3},{4,6},{5,7},{8,10},{9,11},{12,14},{13,15},{16,18},{17,... | collective-permute-start | bytes 196616 | tf_op jit(solution)/shard_map/ppermute | solution.py:507
  113.7 11.0 %collective-permute-start.19 = (f32[128,128]{1,0:T(8,128)S(1)}, f32[128,128]{1,0:T(8,128)S(1)}, u32[]{:S(2)}, u32[]{:S(2)}) collective-permute-start(f32[128,128]{1,0:T(8,128)S(1)} %add.98), channel_id=1, source_target_pairs={{0,2},{1,3},{2,0},{3,1},{4,6},{5,7},{6,4},{7,5},{8,10},{9,11},{10,... | collective-permute-start | bytes 196616 | tf_op jit(solution)/shard_map/ppermute | solution.py:431
  125.3 3.8 %collective-permute-start.22 = (f32[1024,128]{1,0:T(8,128)S(1)}, f32[1024,128]{1,0:T(8,128)S(1)}, u32[]{:S(2)}, u32[]{:S(2)}) collective-permute-start(f32[1024,128]{1,0:T(8,128)S(1)} %collective-permute-done.17), channel_id=1, source_target_pairs={{0,2},{4,6},{9,11},{13,15},{18,16},{22,20},{27,25},{31,29}} | collective-permute-start | bytes 1572872 | tf_op jit(solution)/shard_map/ppermute | solution.py:480
  129.2 22.6 %collective-permute-start.24 = (f32[2048,128]{1,0:T(8,128)S(1)}, f32[2048,128]{1,0:T(8,128)S(1)}, u32[]{:S(2)}, u32[]{:S(2)}) collective-permute-start(f32[2048,128]{1,0:T(8,128)S(1)} %maximum_select_fusion.1.holder_ref), channel_id=1, source_target_pairs={{0,8},{2,10},{4,12},{6,14},{9,1},{11,3},{13,5},{15,7},{16,24},{18,... | collective-permute-start | bytes 3145736 | tf_op jit(solution)/shard_map/ppermute | solution.py:456
  130.5 38.0 %collective-permute-start.23 = (f32[2048,128]{1,0:T(8,128)S(1)}, f32[2048,128]{1,0:T(8,128)S(1)}, u32[]{:S(2)}, u32[]{:S(2)}) collective-permute-start(f32[2048,128]{1,0:T(8,128)S(1)} %maximum_select_fusion.1.holder_ref), channel_id=1, source_target_pairs={{0,4},{2,6},{4,0},{6,2},{9,13},{11,15},{13,9},{15,11},{16,20},{18,... | collective-permute-start | bytes 3145736 | tf_op jit(solution)/shard_map/ppermute | solution.py:456
  151.8 16.8 %collective-permute-start.25 = (f32[2048,128]{1,0:T(8,128)S(1)}, f32[2048,128]{1,0:T(8,128)S(1)}, u32[]{:S(2)}, u32[]{:S(2)}) collective-permute-start(f32[2048,128]{1,0:T(8,128)S(1)} %collective-permute-done.24.other_ref), channel_id=1, source_target_pairs={{1,5},{3,7},{5,1},{7,3},{8,12},{10,14},{12,8},{14,10},{17,21},{19,... | collective-permute-start | bytes 3145736 | tf_op jit(solution)/shard_map/ppermute | solution.py:456
  (8 other events, 33.2 us)

commit v2 on v1

--- a/solution.py
+++ b/solution.py
@@ -117,20 +117,42 @@
     return [ref[i * SUB : (i + 1) * SUB, :] for i in range(ref.shape[0] // SUB)]
 
 
-def first_kernel(gram_ref, panel_ref, factor_ref, inverse_ref, basis_ref, second_ref):
+def split(value):
+    high = value.astype(BF16)
+    return high, (value - high.astype(F32)).astype(BF16)
+
+
+def first_kernel(
+    gram_ref, panel_ref, factor_ref, inverse_ref, basis_out, second_ref, basis_ref, sem
+):
     upper, inverse = cholesky_tiles(tiles_of(gram_ref))
-    factor_ref[...] = jnp.concatenate(upper, axis=0).T
     inverse_ref[...] = jnp.concatenate(inverse, axis=0)
     basis_ref[...] = dot_nt(panel_ref[...], inverse_ref[...])
-    basis = basis_ref[...]
-    second_ref[...] = dot_tn(basis, basis)
+    copy = pltpu.make_async_copy(basis_ref, basis_out, sem)
+    copy.start()
+    factor_ref[...] = jnp.concatenate(upper, axis=0).T
+    high, low = split(basis_ref[...])
+    width = low.shape[1]
+    value = lax.dot_general(
+        high,
+        jnp.concatenate([high, low], axis=1),
+        (((0,), (0,)), ((), ())),
+        preferred_element_type=F32,
+    )
+    cross = value[:, width:]
+    second_ref[...] = value[:, :width] + (cross + cross.T)
+    copy.wait()
 
 
 def first_pass(gram, panel):
     square = jax.ShapeDtypeStruct(gram.shape, F32)
+    near = pl.BlockSpec(memory_space=pltpu.VMEM)
     return pl.pallas_call(
         first_kernel,
         out_shape=(square, square, jax.ShapeDtypeStruct(panel.shape, F32), square),
+        in_specs=[near, near],
+        out_specs=(near, near, pl.BlockSpec(memory_space=pltpu.HBM), near),
+        scratch_shapes=[pltpu.VMEM(panel.shape, F32), pltpu.SemaphoreType.DMA],
         compiler_params=pltpu.CompilerParams(vmem_limit_bytes=24 * 1024 * 1024),
         name="first_pass",
     )(gram, panel)
@@ -172,11 +194,6 @@
     )(upper, inverse, first_factor, top)
 
 
-def split(value):
-    high = value.astype(BF16)
-    return high, (value - high.astype(F32)).astype(BF16)
-
-
 def fetch(away, holder, other, into, sem):
     @pl.when(away == 0)
     def _():
@@ -189,13 +206,9 @@
     return pltpu.make_async_copy(holder, into, sem)
 
 
-def chunk_of(rows):
-    return min(rows, 256)
-
-
 def product_kernel(
     index_ref, trailing, inverse_ref, before_ref, holder_ref, other_ref,
-    out_ref, basis_ref, tiles, panel, both, sem, sems,
+    out_ref, basis_out, tiles, panel, basis_ref, both, sem, sems,
 ):
     slots, chunk, depth = tiles.shape
     rows, width = out_ref.shape
@@ -208,14 +221,17 @@
         return pltpu.make_async_copy(trailing.at[part, columns], tiles.at[slot], sems.at[slot])
 
     fetched = fetch(index_ref[1], holder_ref, other_ref, panel, sem)
-    for i in range(slots):
+    load(0).start()
+    fetched.wait()
+    for i in range(1, slots):
         load(i).start()
 
-    fetched.wait()
     basis_ref[...] = dot_nt(panel[...], inverse_ref[...])
     high, low = split(basis_ref[...])
     both[:, :width] = high
     both[:, width:] = low
+    copy = pltpu.make_async_copy(basis_ref, basis_out, sem)
+    copy.start()
 
     @pl.loop(0, rows // chunk)
     def _(i):
@@ -230,11 +246,13 @@
         def _():
             load(i + slots).start()
 
+    copy.wait()
+
 
 def product(index, trailing, inverse, before, holder, other):
     rows = trailing.shape[0]
     depth, width = holder.shape
-    chunk = chunk_of(rows)
+    chunk = min(rows, 256)
     slots = min(4, rows // chunk)
     anywhere = pl.BlockSpec(memory_space=pl.ANY)
     near = pl.BlockSpec(memory_space=pltpu.VMEM)
@@ -252,9 +270,10 @@
             anywhere,
             anywhere,
         ],
-        out_specs=(near, near),
+        out_specs=(near, pl.BlockSpec(memory_space=pltpu.HBM)),
         scratch_shapes=[
             pltpu.VMEM((slots, chunk, depth), F32),
+            pltpu.VMEM((depth, width), F32),
             pltpu.VMEM((depth, width), F32),
             pltpu.VMEM((depth, 2 * width), BF16),
             pltpu.SemaphoreType.DMA,
@@ -324,8 +343,8 @@
 def update(index, trailing, left, vectors, holder, other, reduced):
     rows = trailing.shape[0]
     depth, width = vectors.shape
-    chunk = chunk_of(rows)
-    slots = min(5, rows // chunk)
+    chunk = min(rows, 256)
+    slots = min(6, rows // chunk)
     anywhere = pl.BlockSpec(memory_space=pl.ANY)
     near = pl.BlockSpec(memory_space=pltpu.VMEM)
     aliases = {}

time: 183 us -> 181 us (0.989)
  Pallas kernels: 68.1 us -> 64.6 us
  starting transfers between devices: 42.7 us -> 44.9 us
    ppermute x14, waiting for transfers between devices: 33.3 us -> 30.3 us  [swap(): return lax.ppermute(value, axis, [(i, i ^ bit) for i in range(count)])]
    ppermute x8, waiting for transfers between devices: 21.1 us -> 23.5 us  [move(): return lax.ppermute(value, ('row', 'col'), pairs)]
where the time goes in v2:
time: 181 us; the launch traced here: 180 us
  Pallas kernels  64.6 us (36%)
  waiting for transfers between devices  55.1 us (30%)
  starting transfers between devices  44.9 us (25%)
  matrix products  7.23 us (4%)
  other arithmetic  3.89 us (2%)
  local copies, waits for them, and re-layouts  3.24 us (2%)
    ppermute x14, waiting for transfers between devices, swap(): return lax.ppermute(value, axis, [(i, i ^ bit) for i in range(count)])  30.3 us
    ppermute x14, starting transfers between devices, swap(): return lax.ppermute(value, axis, [(i, i ^ bit) for i in range(count)])  27.8 us
    pallas_call x2, Pallas kernels, update(): pl.pallas_call(update_kernel, out_shape=jax.ShapeDtypeStruct(trailing.sha...  26.6 us
    ppermute x8, waiting for transfers between devices, move(): return lax.ppermute(value, ('row', 'col'), pairs)  23.5 us
    pallas_call x2, Pallas kernels, product(): pl.pallas_call(product_kernel, out_shape=(jax.ShapeDtypeStruct((rows, wid...  16.9 us
    ppermute x8, starting transfers between devices, move(): return lax.ppermute(value, ('row', 'col'), pairs)  13.4 us
    pallas_call x1, Pallas kernels, small_pass(): pl.pallas_call(small_kernel, out_shape=(square, square), compiler_params=...  7 us
    pallas_call x1, Pallas kernels, first_pass(): pl.pallas_call(first_kernel, out_shape=(square, square, jax.ShapeDtypeStr...  6.34 us
  transfers between devices with their start and end apart: 26, of which 13 were waited for; matrix products, arithmetic and copies ran while one was open for 5% of the time, Pallas kernels for 22%

profile of v2, /device:TPU:12, one launch (start us, length us, event | category | flops | bytes accessed | tf_op | source)
XLA Modules:
  0.0 180.3 jit_solution(7469508932147261696)
XLA Ops:
  5.9 2.8 %collective-permute-done.1 = f32[128,128]{1,0:T(8,128)S(1)} collective-permute-done((f32[128,128]{1,0:T(8,128)S(1)}, f32[128,128]{1,0:T(8,128)S(1)}, u32[]{:S(2)}, u32[]{:S(2)}) %collective-permute-start.1) | collective-permute-done | bytes 65568 | tf_op jit(solution)/shard_map/ppermute | solution.py:450
  9.4 11.7 %collective-permute-start.2 = (f32[128,128]{1,0:T(8,128)S(1)}, f32[128,128]{1,0:T(8,128)S(1)}, u32[]{:S(2)}, u32[]{:S(2)}) collective-permute-start(f32[128,128]{1,0:T(8,128)S(1)} %add.87), channel_id=1, source_target_pairs={{0,8},{4,12},{8,0},{12,4},{16,24},{20,28},{24,16},{28,20},{1,9},{5... | collective-permute-start | bytes 196616 | tf_op jit(solution)/shard_map/ppermute | solution.py:450
  21.1 2.2 %collective-permute-done.2 = f32[128,128]{1,0:T(8,128)S(1)} collective-permute-done((f32[128,128]{1,0:T(8,128)S(1)}, f32[128,128]{1,0:T(8,128)S(1)}, u32[]{:S(2)}, u32[]{:S(2)}) %collective-permute-start.2) | collective-permute-done | bytes 65568 | tf_op jit(solution)/shard_map/ppermute | solution.py:450
  23.9 4.7 %collective-permute-done.3 = f32[128,128]{1,0:T(8,128)S(1)} collective-permute-done((f32[128,128]{1,0:T(8,128)S(1)}, f32[128,128]{1,0:T(8,128)S(1)}, u32[]{:S(2)}, u32[]{:S(2)}) %collective-permute-start.3) | collective-permute-done | bytes 65568 | tf_op jit(solution)/shard_map/ppermute | solution.py:450
  30.0 6.3 %first_pass.1 = (f32[128,128]{1,0:T(8,128)}, f32[128,128]{1,0:T(8,128)S(1)}, f32[2048,128]{1,0:T(8,128)S(1)}, f32[128,128]{1,0:T(8,128)S(1)}) custom-call(f32[128,128]{1,0:T(8,128)S(1)} %add.89.gram_ref, f32[2048,128]{1,0:T(8,128)S(1)} %copy-done), custom_call_target="tpu_custom_call" | custom-call | tf_op jit(solution)/shard_map/first_pass/pallas_call | solution.py:150
  38.9 2.8 %collective-permute-done.6 = f32[128,128]{1,0:T(8,128)S(1)} collective-permute-done((f32[128,128]{1,0:T(8,128)S(1)}, f32[128,128]{1,0:T(8,128)S(1)}, u32[]{:S(2)}, u32[]{:S(2)}) %collective-permute-start.6) | collective-permute-done | bytes 65568 | tf_op jit(solution)/shard_map/ppermute | solution.py:450
  43.3 2.2 %collective-permute-done.5.other_ref = f32[2048,128]{1,0:T(8,128)S(1)} collective-permute-done((f32[2048,128]{1,0:T(8,128)S(1)}, f32[2048,128]{1,0:T(8,128)S(1)}, u32[]{:S(2)}, u32[]{:S(2)}) %collective-permute-start.5) | collective-permute-done | bytes 1048608 | tf_op jit(solution)/shard_map/ppermute | solution.py:475
  45.4 3.4 %collective-permute-start.8 = (f32[2048,128]{1,0:T(8,128)S(1)}, f32[2048,128]{1,0:T(8,128)}, u32[]{:S(2)}, u32[]{:S(2)}) collective-permute-start(f32[2048,128]{1,0:T(8,128)S(1)} %collective-permute-done.5.other_ref), channel_id=1, source_target_pairs={{1,5},{3,7},{5,1},{7,3},{8,12},{10,14},{12,8},{14,10},{17,21},{19,... | collective-permute-start | bytes 3145736 | tf_op jit(solution)/shard_map/ppermute | solution.py:475
  49.8 4.4 %collective-permute-done.9 = f32[128,128]{1,0:T(8,128)S(1)} collective-permute-done((f32[128,128]{1,0:T(8,128)S(1)}, f32[128,128]{1,0:T(8,128)S(1)}, u32[]{:S(2)}, u32[]{:S(2)}) %collective-permute-start.9) | collective-permute-done | bytes 65568 | tf_op jit(solution)/shard_map/ppermute | solution.py:450
  54.9 8.2 %product.2 = (f32[2048,128]{1,0:T(8,128)S(1)}, f32[2048,128]{1,0:T(8,128)S(1)}) custom-call(s32[2]{0:T(128)S(1)} %pad_add_fusion.2.index_ref._, f32[2048,4096]{1,0:T(8,128)} %trailing.7, f32[128,128]{1,0:T(8,128)S(1)} %get-tuple-element.36.inverse_ref, f32[2048,128]{1,0:T(8,128)S(1)} %broadcast_1_before_ref.2.before_ref, ...), custom_call_target="tpu_custom_call" | custom-call | flops 4294967296 | bytes 16777216 | tf_op jit(solution)/shard_map/product/pallas_call | solution.py:259
  64.1 4.1 %second_pass.1 = (f32[128,128]{1,0:T(8,128)S(1)}, f32[128,128]{1,0:T(8,128)S(1)}) custom-call(f32[128,128]{1,0:T(8,128)S(1)} %add.92.gram_ref), custom_call_target="tpu_custom_call" | custom-call | tf_op jit(solution)/shard_map/second_pass/pallas_call | solution.py:169
  68.2 8.8 %product.3 = (f32[2048,128]{1,0:T(8,128)S(1)}, f32[2048,128]{1,0:T(8,128)S(1)}) custom-call(s32[2]{0:T(128)S(1)} %pad_add_fusion.index_ref, f32[2048,4096]{1,0:T(8,128)} %trailing.7, f32[128,128]{1,0:T(8,128)S(1)} %get-tuple-element.36.inverse_ref, f32[2048,128]{1,0:T(8,128)S(1)} %get-tuple-element.41.before_ref, ...), custom_call_target="tpu_custom_call" | custom-call | flops 4294967296 | bytes 16777216 | tf_op jit(solution)/shard_map/product/pallas_call | solution.py:259
  76.9 3.6 %applied.1 = (f32[1024,128]{1,0:T(8,128)S(1)}, f32[1024,128]{1,0:T(8,128)S(1)}, f32[2048,128]{1,0:T(8,128)S(1)}, f32[128,128]{1,0:T(8,128)S(1)}) custom-call(s32[3]{0:T(128)S(1)} %pad_add_fusion.1.index_ref, f32[2048,128]{1,0:T(8,128)S(1)} %get-tuple-element.42.raw_ref, f32[2048,128]{1,0:T(8,128)S(1)} %copy-done.4, ...), custom_call_target="tpu_custom_call" | custom-call | tf_op jit(solution)/shard_map/applied/pallas_call | solution.py:425
  83.4 2.7 %collective-permute-start.12 = (f32[1024,128]{1,0:T(8,128)}, f32[1024,128]{1,0:T(8,128)}, u32[]{:S(2)}, u32[]{:S(2)}) collective-permute-start(f32[1024,128]{1,0:T(8,128)} %add.93), channel_id=1, source_target_pairs={{0,2},{1,3},{2,0},{3,1},{4,6},{5,7},{6,4},{7,5},{8,10},{9,11},{10,... | collective-permute-start | bytes 1572872 | tf_op jit(solution)/shard_map/ppermute | solution.py:450
  86.6 3.7 %collective-permute-done.13 = f32[128,128]{1,0:T(8,128)S(1)} collective-permute-done((f32[128,128]{1,0:T(8,128)S(1)}, f32[128,128]{1,0:T(8,128)S(1)}, u32[]{:S(2)}, u32[]{:S(2)}) %collective-permute-start.13) | collective-permute-done | bytes 65568 | tf_op jit(solution)/shard_map/ppermute | solution.py:450
  91.9 2.8 %collective-permute-done.14 = f32[128,128]{1,0:T(8,128)S(1)} collective-permute-done((f32[128,128]{1,0:T(8,128)S(1)}, f32[128,128]{1,0:T(8,128)S(1)}, u32[]{:S(2)}, u32[]{:S(2)}) %collective-permute-start.14) | collective-permute-done | bytes 65568 | tf_op jit(solution)/shard_map/ppermute | solution.py:450
  96.0 4.0 %collective-permute-done.15 = f32[128,128]{1,0:T(8,128)S(1)} collective-permute-done((f32[128,128]{1,0:T(8,128)S(1)}, f32[128,128]{1,0:T(8,128)S(1)}, u32[]{:S(2)}, u32[]{:S(2)}) %collective-permute-start.15) | collective-permute-done | bytes 65568 | tf_op jit(solution)/shard_map/ppermute | solution.py:450
  106.0 2.3 %collective-permute-start.18 = (f32[128,128]{1,0:T(8,128)S(1)}, f32[128,128]{1,0:T(8,128)S(1)}, u32[]{:S(2)}, u32[]{:S(2)}) collective-permute-start(f32[128,128]{1,0:T(8,128)S(1)} %add.96), channel_id=1, source_target_pairs={{0,1},{1,0},{2,3},{3,2},{4,5},{5,4},{6,7},{7,6},{8,9},{9,8},{10,11... | collective-permute-start | bytes 196616 | tf_op jit(solution)/shard_map/ppermute | solution.py:450
  110.8 2.7 %collective-permute-start.19 = (f32[128,128]{1,0:T(8,128)S(1)}, f32[128,128]{1,0:T(8,128)S(1)}, u32[]{:S(2)}, u32[]{:S(2)}) collective-permute-start(f32[128,128]{1,0:T(8,128)S(1)} %add.98), channel_id=1, source_target_pairs={{0,2},{1,3},{2,0},{3,1},{4,6},{5,7},{6,4},{7,5},{8,10},{9,11},{10,... | collective-permute-start | bytes 196616 | tf_op jit(solution)/shard_map/ppermute | solution.py:450
  114.9 7.0 %small_pass.1 = (f32[128,128]{1,0:T(8,128)}, f32[128,128]{1,0:T(8,128)S(1)}) custom-call(f32[128,128]{1,0:T(8,128)S(1)} %get-tuple-element.52.upper_ref, f32[128,128]{1,0:T(8,128)S(1)} %get-tuple-element.45.inverse_ref, f32[128,128]{1,0:T(8,128)S(1)} %copy-done.5, f32[128,128]{1,0:T(8,128)S(1)} %broadcast_select_fusion.2.top_ref), custom_call_target="tpu_custom_call" | custom-call | tf_op jit(solution)/shard_map/small_pass/pallas_call | solution.py:189
  128.4 21.4 %collective-permute-done.24.other_ref = f32[2048,128]{1,0:T(8,128)S(1)} collective-permute-done((f32[2048,128]{1,0:T(8,128)S(1)}, f32[2048,128]{1,0:T(8,128)S(1)}, u32[]{:S(2)}, u32[]{:S(2)}) %collective-permute-start.24) | collective-permute-done | bytes 1048608 | tf_op jit(solution)/shard_map/ppermute | solution.py:475
  149.8 3.7 %collective-permute-start.25 = (f32[2048,128]{1,0:T(8,128)S(1)}, f32[2048,128]{1,0:T(8,128)S(1)}, u32[]{:S(2)}, u32[]{:S(2)}) collective-permute-start(f32[2048,128]{1,0:T(8,128)S(1)} %collective-permute-done.24.other_ref), channel_id=1, source_target_pairs={{1,5},{3,7},{5,1},{7,3},{8,12},{10,14},{12,8},{14,10},{17,21},{19,... | collective-permute-start | bytes 3145736 | tf_op jit(solution)/shard_map/ppermute | solution.py:475
  153.5 13.3 %update.2._ = f32[2048,4096]{1,0:T(8,128)} custom-call(s32[2]{0:T(128)S(1)} %pad_add_fusion.2.index_ref._, f32[2048,4096]{1,0:T(8,128)} %trailing.7, f32[2048,256]{1,0:T(8,128)S(1)} %pad_maximum_fusion.left_ref, f32[2048,128]{1,0:T(8,128)S(1)} %convolution_add_fusion.1.vectors_ref, f32[2048,128]{1,0:T(8,128)S(1)} %maximum_select_fusion.1.holder_ref, ...), custom_call_target="tpu_custom_call" | custom-call | flops 6442450944 | bytes 33554432 | tf_op jit(solution)/shard_map/update/pallas_call | solution.py:355
  166.8 13.3 %update.3 = f32[2048,4096]{1,0:T(8,128)} custom-call(s32[2]{0:T(128)S(1)} %pad_add_fusion.index_ref, f32[2048,4096]{1,0:T(8,128)} %trailing.7, f32[2048,256]{1,0:T(8,128)S(1)} %pad_maximum_fusion.left_ref, f32[2048,128]{1,0:T(8,128)S(1)} %convolution_add_fusion.vectors_ref, ...), custom_call_target="tpu_custom_call", output_to_operand_aliasing={{}: (6, {})} | custom-call | flops 6442450944 | bytes 33554432 | tf_op jit(solution)/shard_map/update/pallas_call | solution.py:355
  (84 shorter events, 37.0 us)
Async XLA Ops:
  1.8 6.9 %collective-permute-start = (f32[1024,128]{1,0:T(8,128)S(1)}, f32[1024,128]{1,0:T(8,128)S(1)}, u32[]{:S(2)}, u32[]{:S(2)}) collective-permute-start(f32[1024,128]{1,0:T(8,128)S(1)} %constant_dynamic-slice_fusion), channel_id=1, source_target_pairs={{0,16},{2,18},{4,20},{6,22},{9,25},{11,27},{13,29},{15,31},{16,0},... | collective-permute-start | bytes 1572872 | tf_op jit(solution)/shard_map/ppermute | solution.py:475
  4.4 4.3 %collective-permute-start.1 = (f32[128,128]{1,0:T(8,128)S(1)}, f32[128,128]{1,0:T(8,128)S(1)}, u32[]{:S(2)}, u32[]{:S(2)}) collective-permute-start(f32[128,128]{1,0:T(8,128)S(1)} %fusion), channel_id=1, source_target_pairs={{0,4},{4,0},{8,12},{12,8},{16,20},{20,16},{24,28},{28,24},{1,5},{5... | collective-permute-start | bytes 196616 | tf_op jit(solution)/shard_map/ppermute | solution.py:450
  8.7 19.9 %collective-permute-start.4 = (f32[1024,128]{1,0:T(8,128)S(1)}, f32[1024,128]{1,0:T(8,128)S(1)}, u32[]{:S(2)}, u32[]{:S(2)}) collective-permute-start(f32[1024,128]{1,0:T(8,128)S(1)} %collective-permute-done), channel_id=1, source_target_pairs={{0,2},{4,6},{9,11},{13,15},{18,16},{22,20},{27,25},{31,29}} | collective-permute-start | bytes 1572872 | tf_op jit(solution)/shard_map/ppermute | solution.py:499
  9.4 13.9 %collective-permute-start.2 = (f32[128,128]{1,0:T(8,128)S(1)}, f32[128,128]{1,0:T(8,128)S(1)}, u32[]{:S(2)}, u32[]{:S(2)}) collective-permute-start(f32[128,128]{1,0:T(8,128)S(1)} %add.87), channel_id=1, source_target_pairs={{0,8},{4,12},{8,0},{12,4},{16,24},{20,28},{24,16},{28,20},{1,9},{5... | collective-permute-start | bytes 196616 | tf_op jit(solution)/shard_map/ppermute | solution.py:450
  23.4 5.2 %collective-permute-start.3 = (f32[128,128]{1,0:T(8,128)S(1)}, f32[128,128]{1,0:T(8,128)S(1)}, u32[]{:S(2)}, u32[]{:S(2)}) collective-permute-start(f32[128,128]{1,0:T(8,128)S(1)} %add.88), channel_id=1, source_target_pairs={{0,16},{4,20},{8,24},{12,28},{16,0},{20,4},{24,8},{28,12},{1,17},{... | collective-permute-start | bytes 196616 | tf_op jit(solution)/shard_map/ppermute | solution.py:450
  28.7 16.7 %collective-permute-start.5 = (f32[2048,128]{1,0:T(8,128)S(1)}, f32[2048,128]{1,0:T(8,128)S(1)}, u32[]{:S(2)}, u32[]{:S(2)}) collective-permute-start(f32[2048,128]{1,0:T(8,128)S(1)} %maximum_select_fusion.holder_ref), channel_id=1, source_target_pairs={{0,8},{2,10},{4,12},{6,14},{9,1},{11,3},{13,5},{15,7},{16,24},{18,... | collective-permute-start | bytes 3145736 | tf_op jit(solution)/shard_map/ppermute | solution.py:475
  37.4 4.3 %collective-permute-start.6 = (f32[128,128]{1,0:T(8,128)S(1)}, f32[128,128]{1,0:T(8,128)S(1)}, u32[]{:S(2)}, u32[]{:S(2)}) collective-permute-start(f32[128,128]{1,0:T(8,128)S(1)} %get-tuple-element.39), channel_id=1, source_target_pairs={{0,4},{4,0},{8,12},{12,8},{16,20},{20,16},{24,28},{28,24},{1,5},{5... | collective-permute-start | bytes 196616 | tf_op jit(solution)/shard_map/ppermute | solution.py:450
  41.6 26.5 %collective-permute-start.7 = (f32[2048,128]{1,0:T(8,128)S(1)}, f32[2048,128]{1,0:T(8,128)}, u32[]{:S(2)}, u32[]{:S(2)}) collective-permute-start(f32[2048,128]{1,0:T(8,128)S(1)} %maximum_select_fusion.holder_ref), channel_id=1, source_target_pairs={{0,4},{2,6},{4,0},{6,2},{9,13},{11,15},{13,9},{15,11},{16,20},{18,... | collective-permute-start | bytes 3145736 | tf_op jit(solution)/shard_map/ppermute | solution.py:475
  45.4 22.7 %collective-permute-start.8 = (f32[2048,128]{1,0:T(8,128)S(1)}, f32[2048,128]{1,0:T(8,128)}, u32[]{:S(2)}, u32[]{:S(2)}) collective-permute-start(f32[2048,128]{1,0:T(8,128)S(1)} %collective-permute-done.5.other_ref), channel_id=1, source_target_pairs={{1,5},{3,7},{5,1},{7,3},{8,12},{10,14},{12,8},{14,10},{17,21},{19,... | collective-permute-start | bytes 3145736 | tf_op jit(solution)/shard_map/ppermute | solution.py:475
  49.0 5.2 %collective-permute-start.9 = (f32[128,128]{1,0:T(8,128)S(1)}, f32[128,128]{1,0:T(8,128)S(1)}, u32[]{:S(2)}, u32[]{:S(2)}) collective-permute-start(f32[128,128]{1,0:T(8,128)S(1)} %add.90), channel_id=1, source_target_pairs={{0,16},{4,20},{8,24},{12,28},{16,0},{20,4},{24,8},{28,12},{1,17},{... | collective-permute-start | bytes 196616 | tf_op jit(solution)/shard_map/ppermute | solution.py:450
  54.2 9.9 %collective-permute-start.10 = (f32[128,128]{1,0:T(8,128)S(1)}, f32[128,128]{1,0:T(8,128)S(1)}, u32[]{:S(2)}, u32[]{:S(2)}) collective-permute-start(f32[128,128]{1,0:T(8,128)S(1)} %add.91), channel_id=1, source_target_pairs={{0,8},{4,12},{8,0},{12,4},{16,24},{20,28},{24,16},{28,20},{1,9},{5... | collective-permute-start | bytes 196616 | tf_op jit(solution)/shard_map/ppermute | solution.py:450
  83.4 16.6 %collective-permute-start.12 = (f32[1024,128]{1,0:T(8,128)}, f32[1024,128]{1,0:T(8,128)}, u32[]{:S(2)}, u32[]{:S(2)}) collective-permute-start(f32[1024,128]{1,0:T(8,128)} %add.93), channel_id=1, source_target_pairs={{0,2},{1,3},{2,0},{3,1},{4,6},{5,7},{6,4},{7,5},{8,10},{9,11},{10,... | collective-permute-start | bytes 1572872 | tf_op jit(solution)/shard_map/ppermute | solution.py:450
  86.1 4.3 %collective-permute-start.13 = (f32[128,128]{1,0:T(8,128)S(1)}, f32[128,128]{1,0:T(8,128)S(1)}, u32[]{:S(2)}, u32[]{:S(2)}) collective-permute-start(f32[128,128]{1,0:T(8,128)S(1)} %get-tuple-element.48), channel_id=1, source_target_pairs={{0,4},{4,0},{8,12},{12,8},{16,20},{20,16},{24,28},{28,24},{1,5},{5... | collective-permute-start | bytes 196616 | tf_op jit(solution)/shard_map/ppermute | solution.py:450
  90.4 4.3 %collective-permute-start.14 = (f32[128,128]{1,0:T(8,128)S(1)}, f32[128,128]{1,0:T(8,128)S(1)}, u32[]{:S(2)}, u32[]{:S(2)}) collective-permute-start(f32[128,128]{1,0:T(8,128)S(1)} %add.94), channel_id=1, source_target_pairs={{0,8},{4,12},{8,0},{12,4},{16,24},{20,28},{24,16},{28,20},{1,9},{5... | collective-permute-start | bytes 196616 | tf_op jit(solution)/shard_map/ppermute | solution.py:450
  94.7 5.3 %collective-permute-start.15 = (f32[128,128]{1,0:T(8,128)S(1)}, f32[128,128]{1,0:T(8,128)S(1)}, u32[]{:S(2)}, u32[]{:S(2)}) collective-permute-start(f32[128,128]{1,0:T(8,128)S(1)} %add.95), channel_id=1, source_target_pairs={{0,16},{4,20},{8,24},{12,28},{16,0},{20,4},{24,8},{28,12},{1,17},{... | collective-permute-start | bytes 196616 | tf_op jit(solution)/shard_map/ppermute | solution.py:450
  103.4 4.8 %collective-permute-start.20 = (f32[128,128]{1,0:T(8,128)S(1)}, f32[128,128]{1,0:T(8,128)S(1)}, u32[]{:S(2)}, u32[]{:S(2)}) collective-permute-start(f32[128,128]{1,0:T(8,128)S(1)} %select_add_fusion), channel_id=1, source_target_pairs={{0,1},{4,5},{8,9},{12,13},{16,17},{20,21},{24,25},{28,29}} | collective-permute-start | bytes 196616 | tf_op jit(solution)/shard_map/ppermute | solution.py:526
  105.3 16.6 %collective-permute-start.17 = (f32[1024,128]{1,0:T(8,128)S(1)}, f32[1024,128]{1,0:T(8,128)S(1)}, u32[]{:S(2)}, u32[]{:S(2)}) collective-permute-start(f32[1024,128]{1,0:T(8,128)S(1)} %get-tuple-element.67), channel_id=1, source_target_pairs={{0,16},{2,18},{4,20},{6,22},{9,25},{11,27},{13,29},{15,31},{16,0},... | collective-permute-start | bytes 1572872 | tf_op jit(solution)/shard_map/ppermute | solution.py:475
  106.0 4.8 %collective-permute-start.18 = (f32[128,128]{1,0:T(8,128)S(1)}, f32[128,128]{1,0:T(8,128)S(1)}, u32[]{:S(2)}, u32[]{:S(2)}) collective-permute-start(f32[128,128]{1,0:T(8,128)S(1)} %add.96), channel_id=1, source_target_pairs={{0,1},{1,0},{2,3},{3,2},{4,5},{5,4},{6,7},{7,6},{8,9},{9,8},{10,11... | collective-permute-start | bytes 196616 | tf_op jit(solution)/shard_map/ppermute | solution.py:450
  108.3 6.5 %collective-permute-start.21 = (f32[128,128]{1,0:T(8,128)S(1)}, f32[128,128]{1,0:T(8,128)S(1)}, u32[]{:S(2)}, u32[]{:S(2)}) collective-permute-start(f32[128,128]{1,0:T(8,128)S(1)} %broadcast_select_fusion.1), channel_id=1, source_target_pairs={{0,2},{1,3},{4,6},{5,7},{8,10},{9,11},{12,14},{13,15},{16,18},{17,... | collective-permute-start | bytes 196616 | tf_op jit(solution)/shard_map/ppermute | solution.py:526
  110.8 11.0 %collective-permute-start.19 = (f32[128,128]{1,0:T(8,128)S(1)}, f32[128,128]{1,0:T(8,128)S(1)}, u32[]{:S(2)}, u32[]{:S(2)}) collective-permute-start(f32[128,128]{1,0:T(8,128)S(1)} %add.98), channel_id=1, source_target_pairs={{0,2},{1,3},{2,0},{3,1},{4,6},{5,7},{6,4},{7,5},{8,10},{9,11},{10,... | collective-permute-start | bytes 196616 | tf_op jit(solution)/shard_map/ppermute | solution.py:450
  122.4 3.8 %collective-permute-start.22 = (f32[1024,128]{1,0:T(8,128)S(1)}, f32[1024,128]{1,0:T(8,128)S(1)}, u32[]{:S(2)}, u32[]{:S(2)}) collective-permute-start(f32[1024,128]{1,0:T(8,128)S(1)} %collective-permute-done.17), channel_id=1, source_target_pairs={{0,2},{4,6},{9,11},{13,15},{18,16},{22,20},{27,25},{31,29}} | collective-permute-start | bytes 1572872 | tf_op jit(solution)/shard_map/ppermute | solution.py:499
  126.4 23.4 %collective-permute-start.24 = (f32[2048,128]{1,0:T(8,128)S(1)}, f32[2048,128]{1,0:T(8,128)S(1)}, u32[]{:S(2)}, u32[]{:S(2)}) collective-permute-start(f32[2048,128]{1,0:T(8,128)S(1)} %maximum_select_fusion.1.holder_ref), channel_id=1, source_target_pairs={{0,8},{2,10},{4,12},{6,14},{9,1},{11,3},{13,5},{15,7},{16,24},{18,... | collective-permute-start | bytes 3145736 | tf_op jit(solution)/shard_map/ppermute | solution.py:475
  127.7 39.1 %collective-permute-start.23 = (f32[2048,128]{1,0:T(8,128)S(1)}, f32[2048,128]{1,0:T(8,128)S(1)}, u32[]{:S(2)}, u32[]{:S(2)}) collective-permute-start(f32[2048,128]{1,0:T(8,128)S(1)} %maximum_select_fusion.1.holder_ref), channel_id=1, source_target_pairs={{0,4},{2,6},{4,0},{6,2},{9,13},{11,15},{13,9},{15,11},{16,20},{18,... | collective-permute-start | bytes 3145736 | tf_op jit(solution)/shard_map/ppermute | solution.py:475
  149.8 17.0 %collective-permute-start.25 = (f32[2048,128]{1,0:T(8,128)S(1)}, f32[2048,128]{1,0:T(8,128)S(1)}, u32[]{:S(2)}, u32[]{:S(2)}) collective-permute-start(f32[2048,128]{1,0:T(8,128)S(1)} %collective-permute-done.24.other_ref), channel_id=1, source_target_pairs={{1,5},{3,7},{5,1},{7,3},{8,12},{10,14},{12,8},{14,10},{17,21},{19,... | collective-permute-start | bytes 3145736 | tf_op jit(solution)/shard_map/ppermute | solution.py:475
  (8 other events, 32.2 us)

commit v3 on v2

--- a/solution.py
+++ b/solution.py
@@ -123,12 +123,15 @@
 
 
 def first_kernel(
-    gram_ref, panel_ref, factor_ref, inverse_ref, basis_out, second_ref, basis_ref, sem
+    gram_ref, panel, factor_ref, inverse_ref, basis_out, second_ref, panel_ref, basis_ref, sem
 ):
+    fetched = pltpu.make_async_copy(panel, panel_ref, sem.at[0])
+    fetched.start()
     upper, inverse = cholesky_tiles(tiles_of(gram_ref))
     inverse_ref[...] = jnp.concatenate(inverse, axis=0)
+    fetched.wait()
     basis_ref[...] = dot_nt(panel_ref[...], inverse_ref[...])
-    copy = pltpu.make_async_copy(basis_ref, basis_out, sem)
+    copy = pltpu.make_async_copy(basis_ref, basis_out, sem.at[1])
     copy.start()
     factor_ref[...] = jnp.concatenate(upper, axis=0).T
     high, low = split(basis_ref[...])
@@ -150,9 +153,13 @@
     return pl.pallas_call(
         first_kernel,
         out_shape=(square, square, jax.ShapeDtypeStruct(panel.shape, F32), square),
-        in_specs=[near, near],
+        in_specs=[near, pl.BlockSpec(memory_space=pl.ANY)],
         out_specs=(near, near, pl.BlockSpec(memory_space=pltpu.HBM), near),
-        scratch_shapes=[pltpu.VMEM(panel.shape, F32), pltpu.SemaphoreType.DMA],
+        scratch_shapes=[
+            pltpu.VMEM(panel.shape, F32),
+            pltpu.VMEM(panel.shape, F32),
+            pltpu.SemaphoreType.DMA((2,)),
+        ],
         compiler_params=pltpu.CompilerParams(vmem_limit_bytes=24 * 1024 * 1024),
         name="first_pass",
     )(gram, panel)
@@ -287,36 +294,45 @@
     )(index, trailing, inverse, before, holder, other)
 
 
-def update_kernel(
-    index_ref, trailing, left_ref, vectors_ref, holder_ref, other_ref, _,
-    out, tiles, applied, right, sem, loads, stores,
-):
+def update_kernel(count_left, has_vectors, has_applied, index_ref, source, *refs):
+    lefts, refs = refs[:count_left], list(refs[count_left:])
+    vectors_ref = refs.pop(0) if has_vectors else None
+    holder_ref, other_ref = (refs.pop(0), refs.pop(0)) if has_applied else (None, None)
+    _, out, tiles, right, applied, sem, loads, stores = refs
     slots, chunk, depth = tiles.shape
-    rows, width = left_ref.shape[0], vectors_ref.shape[1]
+    rows, width = lefts[0].shape
     count = rows // chunk
     ahead = max(slots - 2, 1)
     columns = pl.ds(pl.multiple_of(index_ref[0] * depth, depth), depth)
 
+    def place(array, i):
+        part = pl.ds(pl.multiple_of(i * chunk, chunk), chunk)
+        return array.at[part, columns] if array.shape[1] > depth else array.at[part]
+
     def load(i):
-        part = pl.ds(pl.multiple_of(i * chunk, chunk), chunk)
         slot = i % slots
-        return pltpu.make_async_copy(trailing.at[part, columns], tiles.at[slot], loads.at[slot])
+        return pltpu.make_async_copy(place(source, i), tiles.at[slot], loads.at[slot])
 
     def store(i):
-        part = pl.ds(pl.multiple_of(i * chunk, chunk), chunk)
         slot = i % slots
-        return pltpu.make_async_copy(tiles.at[slot], out.at[part, columns], stores.at[slot])
-
-    fetched = fetch(index_ref[1], holder_ref, other_ref, applied, sem)
+        return pltpu.make_async_copy(tiles.at[slot], place(out, i), stores.at[slot])
+
+    if has_applied:
+        fetched = fetch(index_ref[1], holder_ref, other_ref, applied, sem)
     for i in range(min(ahead, count)):
         load(i).start()
 
-    fetched.wait()
-    for place, ref in ((0, applied), (width, vectors_ref)):
+    pieces = []
+    if has_applied:
+        fetched.wait()
+        pieces.append(applied)
+    if has_vectors:
+        pieces.append(vectors_ref)
+    for n, ref in enumerate(pieces):
         high, low = split(ref[...].T)
-        right[place : place + width, :] = high
-        right[2 * width + place : 3 * width + place, :] = low
-        right[4 * width + place : 5 * width + place, :] = high
+        for term, value in enumerate((high, low, high)):
+            start = (term * count_left + n) * width
+            right[start : start + width, :] = value
 
     @pl.loop(0, count)
     def _(i):
@@ -330,8 +346,9 @@
 
         load(i).wait()
         part = pl.ds(pl.multiple_of(i * chunk, chunk), chunk)
-        high, low = split(left_ref[part, :])
-        left = jnp.concatenate([high, high, low], axis=1)
+        terms = [split(ref[part, :]) for ref in lefts]
+        high, low = [value for value, _ in terms], [value for _, value in terms]
+        left = jnp.concatenate(high + high + low, axis=1)
         slot = i % slots
         tiles[slot] = tiles[slot] - dot_fast(left, right[...])
         store(i).start()
@@ -340,46 +357,46 @@
         store(i).wait()
 
 
-def update(index, trailing, left, vectors, holder, other, reduced):
-    rows = trailing.shape[0]
-    depth, width = vectors.shape
+def update(index, source, lefts, vectors, applied, reduced, out_columns):
+    rows, width = lefts[0].shape
+    depth = (applied[0] if vectors is None else vectors).shape[0]
     chunk = min(rows, 256)
     slots = min(6, rows // chunk)
     anywhere = pl.BlockSpec(memory_space=pl.ANY)
     near = pl.BlockSpec(memory_space=pltpu.VMEM)
-    aliases = {}
-    if reduced is None:
-        reduced = index
-    else:
-        aliases = {6: 0}
+    operands = [index, source, *lefts]
+    specs = [pl.BlockSpec(memory_space=pltpu.SMEM), anywhere, *[near for _ in lefts]]
+    if vectors is not None:
+        operands.append(vectors)
+        specs.append(near)
+    if applied is not None:
+        operands += applied
+        specs += [anywhere, anywhere]
+    aliases = {} if reduced is None else {len(operands): 0}
+    operands.append(index if reduced is None else reduced)
+    specs.append(anywhere)
     return pl.pallas_call(
-        update_kernel,
-        out_shape=jax.ShapeDtypeStruct(trailing.shape, F32),
-        in_specs=[
-            pl.BlockSpec(memory_space=pltpu.SMEM),
-            anywhere,
-            near,
-            near,
-            anywhere,
-            anywhere,
-            anywhere,
-        ],
+        functools.partial(update_kernel, len(lefts), vectors is not None, applied is not None),
+        out_shape=jax.ShapeDtypeStruct((rows, out_columns), F32),
+        in_specs=specs,
         out_specs=anywhere,
         scratch_shapes=[
             pltpu.VMEM((slots, chunk, depth), F32),
+            pltpu.VMEM((3 * len(lefts) * width, depth), BF16),
             pltpu.VMEM((depth, width), F32),
-            pltpu.VMEM((6 * width, depth), BF16),
             pltpu.SemaphoreType.DMA,
             pltpu.SemaphoreType.DMA((slots,)),
             pltpu.SemaphoreType.DMA((slots,)),
         ],
         input_output_aliases=aliases,
-        compiler_params=pltpu.CompilerParams(vmem_limit_bytes=30 * 1024 * 1024),
+        compiler_params=pltpu.CompilerParams(vmem_limit_bytes=24 * 1024 * 1024),
         cost_estimate=pl.CostEstimate(
-            flops=12 * rows * depth * width, bytes_accessed=8 * rows * depth, transcendentals=0
+            flops=6 * len(lefts) * rows * depth * width,
+            bytes_accessed=8 * rows * depth,
+            transcendentals=0,
         ),
         name="update",
-    )(index, trailing, left, vectors, holder, other, reduced)
+    )(*operands)
 
 
 def dot_three(a, b, dims):
@@ -591,20 +608,30 @@
     inner = sum_small(after(inner, piece), "col", col_bits)
     relayed, (inner, kernel) = gather.relay_halves(applied, piece, (inner, kernel))
     inner = dot_tn(kernel, dot_nn(inner, kernel))
-    left = jnp.concatenate(
-        [dot_nt(vectors, kernel), dot_nn(applied, kernel) - dot_nn(vectors, inner)], axis=1
-    )
+    lefts = [dot_nt(vectors, kernel), dot_nn(applied, kernel) - dot_nn(vectors, inner)]
     block_vectors = [
-        dot_nt(basis, second_inverse) + identity_rows((col * ratio + (part ^ low)) * shard_rows)
+        dot_nt(after(basis, kernel), second_inverse)
+        + identity_rows((col * ratio + (part ^ low)) * shard_rows)
         for part, basis in enumerate(bases)
     ]
-    relayed, left, *block_vectors = lax.optimization_barrier((relayed, left, *block_vectors))
+    relayed, *lefts = lax.optimization_barrier((relayed, *lefts, *block_vectors))
+    lefts, block_vectors = lefts[:2], lefts[2:]
     moved_high, moved_low = gather.near(relayed)
+    columns = trailing.shape[1]
+
+    last = ratio - 1
+    started = update(
+        index_of(last), trailing, lefts[1:], block_vectors[last], None, None, shard_rows
+    )
+    moved_high, started = lax.optimization_barrier((moved_high, started))
     parts = [(relayed, moved_high), (moved_low, gather.across(moved_high))]
-    reduced = update(index_of(0), trailing, left, block_vectors[0], *parts[0], None)
     parts += gather.rest(parts)
-    for part in range(1, ratio):
-        reduced = update(index_of(part), trailing, left, block_vectors[part], *parts[part], reduced)
+    reduced = None
+    for part in range(last):
+        reduced = update(
+            index_of(part), trailing, lefts, block_vectors[part], parts[part], reduced, columns
+        )
+    reduced = update(index_of(last), started, lefts[:1], None, parts[last], reduced, columns)
     return (reduced, band_block, first_factor)
 
 

time: 181 us -> 180 us (level)
  waiting for transfers between devices: 55.1 us -> 43.9 us
  Pallas kernels: 64.6 us -> 71.7 us
  matrix products: 7.23 us -> 9.99 us
  starting transfers between devices: 44.9 us -> 42.2 us
  local copies, waits for them, and re-layouts: 3.24 us -> 5.39 us
    ppermute x8, waiting for transfers between devices: 23.5 us -> 9.17 us  [move(): return lax.ppermute(value, ('row', 'col'), pairs)]
    pallas_call x2 -> x3, Pallas kernels: 26.6 us -> 32.8 us  [update(): pl.pallas_call(functools.partial(update_kernel, len(lefts), vectors is no...]
    ppermute x14, starting transfers between devices: 27.8 us -> 25.1 us  [swap(): return lax.ppermute(value, axis, [(i, i ^ bit) for i in range(count)])]
    ppermute x14, waiting for transfers between devices: 30.3 us -> 32.3 us  [swap(): return lax.ppermute(value, axis, [(i, i ^ bit) for i in range(count)])]
  transfers between devices with their start and end apart: 26 -> 26, of which waited for: 13 -> 14; matrix products, arithmetic and copies ran while one was open for 5% -> 7% of each run, Pallas kernels for 22% -> 28%
where the time goes in v3:
time: 180 us; the launch traced here: 179 us
  Pallas kernels  71.7 us (40%)
  waiting for transfers between devices  43.9 us (24%)
  starting transfers between devices  42.2 us (23%)
  matrix products  9.99 us (6%)
  local copies, waits for them, and re-layouts  5.39 us (3%)
  other arithmetic  4.92 us (3%)
    pallas_call x3, Pallas kernels, update(): pl.pallas_call(functools.partial(update_kernel, len(lefts), vectors is no...  32.8 us
    ppermute x14, waiting for transfers between devices, swap(): return lax.ppermute(value, axis, [(i, i ^ bit) for i in range(count)])  32.3 us
    ppermute x14, starting transfers between devices, swap(): return lax.ppermute(value, axis, [(i, i ^ bit) for i in range(count)])  25.1 us
    pallas_call x2, Pallas kernels, product(): pl.pallas_call(product_kernel, out_shape=(jax.ShapeDtypeStruct((rows, wid...  17.7 us
    ppermute x8, starting transfers between devices, move(): return lax.ppermute(value, ('row', 'col'), pairs)  13.5 us
    ppermute x8, waiting for transfers between devices, move(): return lax.ppermute(value, ('row', 'col'), pairs)  9.17 us
    pallas_call x1, Pallas kernels, small_pass(): pl.pallas_call(small_kernel, out_shape=(square, square), compiler_params=...  7 us
    pallas_call x1, Pallas kernels, first_pass(): pl.pallas_call(first_kernel, out_shape=(square, square, jax.ShapeDtypeStr...  6.47 us
  transfers between devices with their start and end apart: 26, of which 14 were waited for; matrix products, arithmetic and copies ran while one was open for 7% of the time, Pallas kernels for 28%

profile of v3, /device:TPU:12, one launch (start us, length us, event | category | flops | bytes accessed | tf_op | source)
XLA Modules:
  0.0 179.4 jit_solution(452206055269972738)
XLA Ops:
  2.4 3.4 %fusion = f32[128,128]{1,0:T(8,128)S(1)} fusion(f32[2048,128]{1,0:T(8,128)} %panel.1), kind=kOutput, calls=%fused_computation.19 | convolution fusion | flops 402653184 | bytes 1114112 | tf_op jit(solution)/shard_map/dot_general | solution.py:25
  7.4 2.8 %collective-permute-done.1 = f32[128,128]{1,0:T(8,128)S(1)} collective-permute-done((f32[128,128]{1,0:T(8,128)S(1)}, f32[128,128]{1,0:T(8,128)S(1)}, u32[]{:S(2)}, u32[]{:S(2)}) %collective-permute-start.1) | collective-permute-done | bytes 65568 | tf_op jit(solution)/shard_map/ppermute | solution.py:467
  10.9 10.2 %collective-permute-start.2 = (f32[128,128]{1,0:T(8,128)S(1)}, f32[128,128]{1,0:T(8,128)S(1)}, u32[]{:S(2)}, u32[]{:S(2)}) collective-permute-start(f32[128,128]{1,0:T(8,128)S(1)} %add.87), channel_id=1, source_target_pairs={{0,8},{4,12},{8,0},{12,4},{16,24},{20,28},{24,16},{28,20},{1,9},{5... | collective-permute-start | bytes 196616 | tf_op jit(solution)/shard_map/ppermute | solution.py:467
  23.8 4.7 %collective-permute-done.3 = f32[128,128]{1,0:T(8,128)S(1)} collective-permute-done((f32[128,128]{1,0:T(8,128)S(1)}, f32[128,128]{1,0:T(8,128)S(1)}, u32[]{:S(2)}, u32[]{:S(2)}) %collective-permute-start.3) | collective-permute-done | bytes 65568 | tf_op jit(solution)/shard_map/ppermute | solution.py:467
  32.4 6.5 %first_pass.1 = (f32[128,128]{1,0:T(8,128)}, f32[128,128]{1,0:T(8,128)S(1)}, f32[2048,128]{1,0:T(8,128)S(1)}, f32[128,128]{1,0:T(8,128)S(1)}) custom-call(f32[128,128]{1,0:T(8,128)S(1)} %add.89.gram_ref, f32[2048,128]{1,0:T(8,128)S(1)} %copy-done), custom_call_target="tpu_custom_call" | custom-call | tf_op jit(solution)/shard_map/first_pass/pallas_call | solution.py:153
  41.4 3.0 %collective-permute-done.6 = f32[128,128]{1,0:T(8,128)S(1)} collective-permute-done((f32[128,128]{1,0:T(8,128)S(1)}, f32[128,128]{1,0:T(8,128)S(1)}, u32[]{:S(2)}, u32[]{:S(2)}) %collective-permute-start.6) | collective-permute-done | bytes 65568 | tf_op jit(solution)/shard_map/ppermute | solution.py:467
  46.7 3.4 %collective-permute-start.8 = (f32[2048,128]{1,0:T(8,128)}, f32[2048,128]{1,0:T(8,128)}, u32[]{:S(2)}, u32[]{:S(2)}) collective-permute-start(f32[2048,128]{1,0:T(8,128)} %collective-permute-done.5.other_ref), channel_id=1, source_target_pairs={{1,5},{3,7},{5,1},{7,3},{8,12},{10,14},{12,8},{14,10},{17,21},{19,... | collective-permute-start | bytes 3145736 | tf_op jit(solution)/shard_map/ppermute | solution.py:492
  51.0 4.4 %collective-permute-done.9 = f32[128,128]{1,0:T(8,128)S(1)} collective-permute-done((f32[128,128]{1,0:T(8,128)S(1)}, f32[128,128]{1,0:T(8,128)S(1)}, u32[]{:S(2)}, u32[]{:S(2)}) %collective-permute-start.9) | collective-permute-done | bytes 65568 | tf_op jit(solution)/shard_map/ppermute | solution.py:467
  55.4 2.8 %collective-permute-start.10 = (f32[128,128]{1,0:T(8,128)S(1)}, f32[128,128]{1,0:T(8,128)S(1)}, u32[]{:S(2)}, u32[]{:S(2)}) collective-permute-start(f32[128,128]{1,0:T(8,128)S(1)} %add.91), channel_id=1, source_target_pairs={{0,8},{4,12},{8,0},{12,4},{16,24},{20,28},{24,16},{28,20},{1,9},{5... | collective-permute-start | bytes 196616 | tf_op jit(solution)/shard_map/ppermute | solution.py:467
  58.3 9.0 %product.2 = (f32[2048,128]{1,0:T(8,128)S(1)}, f32[2048,128]{1,0:T(8,128)S(1)}) custom-call(s32[2]{0:T(128)S(1)} %pad_add_fusion.2.index_ref.refs_5_, f32[2048,4096]{1,0:T(8,128)} %source.3, f32[128,128]{1,0:T(8,128)S(1)} %get-tuple-element.41.inverse_ref, f32[2048,128]{1,0:T(8,128)S(1)} %broadcast_1_before_ref.2.before_ref, ...), custom_call_target="tpu_custom_call" | custom-call | flops 4294967296 | bytes 16777216 | tf_op jit(solution)/shard_map/product/pallas_call | solution.py:266
  67.3 4.1 %second_pass.1 = (f32[128,128]{1,0:T(8,128)S(1)}, f32[128,128]{1,0:T(8,128)S(1)}) custom-call(f32[128,128]{1,0:T(8,128)S(1)} %add.92.gram_ref), custom_call_target="tpu_custom_call" | custom-call | tf_op jit(solution)/shard_map/second_pass/pallas_call | solution.py:176
  71.4 8.8 %product.3 = (f32[2048,128]{1,0:T(8,128)S(1)}, f32[2048,128]{1,0:T(8,128)S(1)}) custom-call(s32[2]{0:T(128)S(1)} %pad_add_fusion.index_ref.refs_2_, f32[2048,4096]{1,0:T(8,128)} %source.3, f32[128,128]{1,0:T(8,128)S(1)} %get-tuple-element.41.inverse_ref, f32[2048,128]{1,0:T(8,128)S(1)} %get-tuple-element.46.before_ref, ...), custom_call_target="tpu_custom_call" | custom-call | flops 4294967296 | bytes 16777216 | tf_op jit(solution)/shard_map/product/pallas_call | solution.py:266
  81.2 3.6 %applied.1 = (f32[1024,128]{1,0:T(8,128)S(1)}, f32[1024,128]{1,0:T(8,128)S(1)}, f32[2048,128]{1,0:T(8,128)S(1)}, f32[128,128]{1,0:T(8,128)S(1)}) custom-call(s32[3]{0:T(128)S(1)} %pad_add_fusion.1.index_ref, f32[2048,128]{1,0:T(8,128)S(1)} %get-tuple-element.47.raw_ref, f32[2048,128]{1,0:T(8,128)S(1)} %copy-done.3, ...), custom_call_target="tpu_custom_call" | custom-call | tf_op jit(solution)/shard_map/applied/pallas_call | solution.py:442
  86.9 2.7 %collective-permute-start.12 = (f32[1024,128]{1,0:T(8,128)S(1)}, f32[1024,128]{1,0:T(8,128)S(1)}, u32[]{:S(2)}, u32[]{:S(2)}) collective-permute-start(f32[1024,128]{1,0:T(8,128)S(1)} %add.93), channel_id=1, source_target_pairs={{0,2},{1,3},{2,0},{3,1},{4,6},{5,7},{6,4},{7,5},{8,10},{9,11},{10,... | collective-permute-start | bytes 1572872 | tf_op jit(solution)/shard_map/ppermute | solution.py:467
  90.1 3.7 %collective-permute-done.13 = f32[128,128]{1,0:T(8,128)S(1)} collective-permute-done((f32[128,128]{1,0:T(8,128)S(1)}, f32[128,128]{1,0:T(8,128)S(1)}, u32[]{:S(2)}, u32[]{:S(2)}) %collective-permute-start.13) | collective-permute-done | bytes 65568 | tf_op jit(solution)/shard_map/ppermute | solution.py:467
  93.9 4.3 %collective-permute-done.14 = f32[128,128]{1,0:T(8,128)S(1)} collective-permute-done((f32[128,128]{1,0:T(8,128)S(1)}, f32[128,128]{1,0:T(8,128)S(1)}, u32[]{:S(2)}, u32[]{:S(2)}) %collective-permute-start.14) | collective-permute-done | bytes 65568 | tf_op jit(solution)/shard_map/ppermute | solution.py:467
  98.4 5.0 %collective-permute-done.15 = f32[128,128]{1,0:T(8,128)S(1)} collective-permute-done((f32[128,128]{1,0:T(8,128)S(1)}, f32[128,128]{1,0:T(8,128)S(1)}, u32[]{:S(2)}, u32[]{:S(2)}) %collective-permute-start.15) | collective-permute-done | bytes 65568 | tf_op jit(solution)/shard_map/ppermute | solution.py:467
  112.3 2.7 %collective-permute-start.19 = (f32[128,128]{1,0:T(8,128)S(1)}, f32[128,128]{1,0:T(8,128)S(1)}, u32[]{:S(2)}, u32[]{:S(2)}) collective-permute-start(f32[128,128]{1,0:T(8,128)S(1)} %add.98), channel_id=1, source_target_pairs={{0,2},{1,3},{2,0},{3,1},{4,6},{5,7},{6,4},{7,5},{8,10},{9,11},{10,... | collective-permute-start | bytes 196616 | tf_op jit(solution)/shard_map/ppermute | solution.py:467
  117.5 7.0 %small_pass.1 = (f32[128,128]{1,0:T(8,128)}, f32[128,128]{1,0:T(8,128)S(1)}) custom-call(f32[128,128]{1,0:T(8,128)S(1)} %get-tuple-element.57.upper_ref, f32[128,128]{1,0:T(8,128)S(1)} %get-tuple-element.50.inverse_ref, f32[128,128]{1,0:T(8,128)S(1)} %copy-done.4, f32[128,128]{1,0:T(8,128)S(1)} %broadcast_select_fusion.2.top_ref), custom_call_target="tpu_custom_call" | custom-call | tf_op jit(solution)/shard_map/small_pass/pallas_call | solution.py:196
  134.1 9.7 %update.3.source = f32[2048,2048]{1,0:T(8,128)S(1)} custom-call(s32[2]{0:T(128)S(1)} %pad_add_fusion.index_ref.refs_2_, f32[2048,4096]{1,0:T(8,128)} %source.3, f32[2048,128]{1,0:T(8,128)S(1)} %convolution_subtract_fusion.refs_0_.refs_1_, f32[2048,128]{1,0:T(8,128)S(1)} %convolution_add_fusion.refs_1_, s32[2]{0:T(128)S(1)} %pad_add_fusion.index_ref.refs_2_), custom_call_target="tpu_custom_call" | custom-call | flops 3221225472 | bytes 33554432 | tf_op jit(solution)/shard_map/update/pallas_call | solution.py:378
  143.8 8.5 %collective-permute-done.23.refs_4_ = f32[2048,128]{1,0:T(8,128)S(1)} collective-permute-done((f32[2048,128]{1,0:T(8,128)S(1)}, f32[2048,128]{1,0:T(8,128)S(1)}, u32[]{:S(2)}, u32[]{:S(2)}) %collective-permute-start.23) | collective-permute-done | bytes 1048608 | tf_op jit(solution)/shard_map/ppermute | solution.py:492
  152.3 3.8 %collective-permute-start.25 = (f32[2048,128]{1,0:T(8,128)S(1)}, f32[2048,128]{1,0:T(8,128)S(1)}, u32[]{:S(2)}, u32[]{:S(2)}) collective-permute-start(f32[2048,128]{1,0:T(8,128)S(1)} %collective-permute-done.23.refs_4_), channel_id=1, source_target_pairs={{1,5},{3,7},{5,1},{7,3},{8,12},{10,14},{12,8},{14,10},{17,21},{19,... | collective-permute-start | bytes 3145736 | tf_op jit(solution)/shard_map/ppermute | solution.py:492
  156.0 13.3 %update.4.refs_3_ = f32[2048,4096]{1,0:T(8,128)} custom-call(s32[2]{0:T(128)S(1)} %pad_add_fusion.2.index_ref.refs_5_, f32[2048,4096]{1,0:T(8,128)} %source.3, f32[2048,128]{1,0:T(8,128)S(1)} %fusion.1.refs_0_, f32[2048,128]{1,0:T(8,128)S(1)} %convolution_subtract_fusion.refs_0_.refs_1_, f32[2048,128]{1,0:T(8,128)S(1)} %convolution_add_fusion.1.refs_2_, ...), custom_call_target="tpu_custom_call" | custom-call | flops 6442450944 | bytes 33554432 | tf_op jit(solution)/shard_map/update/pallas_call | solution.py:378
  169.4 9.8 %update.5 = f32[2048,4096]{1,0:T(8,128)} custom-call(s32[2]{0:T(128)S(1)} %pad_add_fusion.index_ref.refs_2_, f32[2048,2048]{1,0:T(8,128)S(1)} %update.3.source, f32[2048,128]{1,0:T(8,128)S(1)} %fusion.1.refs_0_, f32[2048,128]{1,0:T(8,128)S(1)} %collective-permute-done.24.refs_1_, ...), custom_call_target="tpu_custom_call", output_to_operand_aliasing={{}: (5, {})} | custom-call | flops 3221225472 | bytes 33554432 | tf_op jit(solution)/shard_map/update/pallas_call | solution.py:378
  (82 shorter events, 41.2 us)
Async XLA Ops:
  1.7 8.4 %collective-permute-start = (f32[1024,128]{1,0:T(8,128)S(1)}, f32[1024,128]{1,0:T(8,128)S(1)}, u32[]{:S(2)}, u32[]{:S(2)}) collective-permute-start(f32[1024,128]{1,0:T(8,128)S(1)} %constant_dynamic-slice_fusion), channel_id=1, source_target_pairs={{0,16},{2,18},{4,20},{6,22},{9,25},{11,27},{13,29},{15,31},{16,0},... | collective-permute-start | bytes 1572872 | tf_op jit(solution)/shard_map/ppermute | solution.py:492
  5.8 4.3 %collective-permute-start.1 = (f32[128,128]{1,0:T(8,128)S(1)}, f32[128,128]{1,0:T(8,128)S(1)}, u32[]{:S(2)}, u32[]{:S(2)}) collective-permute-start(f32[128,128]{1,0:T(8,128)S(1)} %fusion), channel_id=1, source_target_pairs={{0,4},{4,0},{8,12},{12,8},{16,20},{20,16},{24,28},{28,24},{1,5},{5... | collective-permute-start | bytes 196616 | tf_op jit(solution)/shard_map/ppermute | solution.py:467
  10.2 18.4 %collective-permute-start.4 = (f32[1024,128]{1,0:T(8,128)S(1)}, f32[1024,128]{1,0:T(8,128)S(1)}, u32[]{:S(2)}, u32[]{:S(2)}) collective-permute-start(f32[1024,128]{1,0:T(8,128)S(1)} %collective-permute-done), channel_id=1, source_target_pairs={{0,2},{4,6},{9,11},{13,15},{18,16},{22,20},{27,25},{31,29}} | collective-permute-start | bytes 1572872 | tf_op jit(solution)/shard_map/ppermute | solution.py:516
  10.9 12.4 %collective-permute-start.2 = (f32[128,128]{1,0:T(8,128)S(1)}, f32[128,128]{1,0:T(8,128)S(1)}, u32[]{:S(2)}, u32[]{:S(2)}) collective-permute-start(f32[128,128]{1,0:T(8,128)S(1)} %add.87), channel_id=1, source_target_pairs={{0,8},{4,12},{8,0},{12,4},{16,24},{20,28},{24,16},{28,20},{1,9},{5... | collective-permute-start | bytes 196616 | tf_op jit(solution)/shard_map/ppermute | solution.py:467
  23.3 5.2 %collective-permute-start.3 = (f32[128,128]{1,0:T(8,128)S(1)}, f32[128,128]{1,0:T(8,128)S(1)}, u32[]{:S(2)}, u32[]{:S(2)}) collective-permute-start(f32[128,128]{1,0:T(8,128)S(1)} %add.88), channel_id=1, source_target_pairs={{0,16},{4,20},{8,24},{12,28},{16,0},{20,4},{24,8},{28,12},{1,17},{... | collective-permute-start | bytes 196616 | tf_op jit(solution)/shard_map/ppermute | solution.py:467
  29.9 16.8 %collective-permute-start.5 = (f32[2048,128]{1,0:T(8,128)S(1)}, f32[2048,128]{1,0:T(8,128)}, u32[]{:S(2)}, u32[]{:S(2)}) collective-permute-start(f32[2048,128]{1,0:T(8,128)S(1)} %maximum_select_fusion.holder_ref), channel_id=1, source_target_pairs={{0,8},{2,10},{4,12},{6,14},{9,1},{11,3},{13,5},{15,7},{16,24},{18,... | collective-permute-start | bytes 3145736 | tf_op jit(solution)/shard_map/ppermute | solution.py:492
  39.9 4.5 %collective-permute-start.6 = (f32[128,128]{1,0:T(8,128)S(1)}, f32[128,128]{1,0:T(8,128)S(1)}, u32[]{:S(2)}, u32[]{:S(2)}) collective-permute-start(f32[128,128]{1,0:T(8,128)S(1)} %get-tuple-element.44), channel_id=1, source_target_pairs={{0,4},{4,0},{8,12},{12,8},{16,20},{20,16},{24,28},{28,24},{1,5},{5... | collective-permute-start | bytes 196616 | tf_op jit(solution)/shard_map/ppermute | solution.py:467
  44.4 27.0 %collective-permute-start.7 = (f32[2048,128]{1,0:T(8,128)S(1)}, f32[2048,128]{1,0:T(8,128)}, u32[]{:S(2)}, u32[]{:S(2)}) collective-permute-start(f32[2048,128]{1,0:T(8,128)S(1)} %maximum_select_fusion.holder_ref), channel_id=1, source_target_pairs={{0,4},{2,6},{4,0},{6,2},{9,13},{11,15},{13,9},{15,11},{16,20},{18,... | collective-permute-start | bytes 3145736 | tf_op jit(solution)/shard_map/ppermute | solution.py:492
  46.7 24.7 %collective-permute-start.8 = (f32[2048,128]{1,0:T(8,128)}, f32[2048,128]{1,0:T(8,128)}, u32[]{:S(2)}, u32[]{:S(2)}) collective-permute-start(f32[2048,128]{1,0:T(8,128)} %collective-permute-done.5.other_ref), channel_id=1, source_target_pairs={{1,5},{3,7},{5,1},{7,3},{8,12},{10,14},{12,8},{14,10},{17,21},{19,... | collective-permute-start | bytes 3145736 | tf_op jit(solution)/shard_map/ppermute | solution.py:492
  50.3 5.2 %collective-permute-start.9 = (f32[128,128]{1,0:T(8,128)S(1)}, f32[128,128]{1,0:T(8,128)S(1)}, u32[]{:S(2)}, u32[]{:S(2)}) collective-permute-start(f32[128,128]{1,0:T(8,128)S(1)} %add.90), channel_id=1, source_target_pairs={{0,16},{4,20},{8,24},{12,28},{16,0},{20,4},{24,8},{28,12},{1,17},{... | collective-permute-start | bytes 196616 | tf_op jit(solution)/shard_map/ppermute | solution.py:467
  55.4 11.8 %collective-permute-start.10 = (f32[128,128]{1,0:T(8,128)S(1)}, f32[128,128]{1,0:T(8,128)S(1)}, u32[]{:S(2)}, u32[]{:S(2)}) collective-permute-start(f32[128,128]{1,0:T(8,128)S(1)} %add.91), channel_id=1, source_target_pairs={{0,8},{4,12},{8,0},{12,4},{16,24},{20,28},{24,16},{28,20},{1,9},{5... | collective-permute-start | bytes 196616 | tf_op jit(solution)/shard_map/ppermute | solution.py:467
  86.9 16.6 %collective-permute-start.12 = (f32[1024,128]{1,0:T(8,128)S(1)}, f32[1024,128]{1,0:T(8,128)S(1)}, u32[]{:S(2)}, u32[]{:S(2)}) collective-permute-start(f32[1024,128]{1,0:T(8,128)S(1)} %add.93), channel_id=1, source_target_pairs={{0,2},{1,3},{2,0},{3,1},{4,6},{5,7},{6,4},{7,5},{8,10},{9,11},{10,... | collective-permute-start | bytes 1572872 | tf_op jit(solution)/shard_map/ppermute | solution.py:467
  89.6 4.3 %collective-permute-start.13 = (f32[128,128]{1,0:T(8,128)S(1)}, f32[128,128]{1,0:T(8,128)S(1)}, u32[]{:S(2)}, u32[]{:S(2)}) collective-permute-start(f32[128,128]{1,0:T(8,128)S(1)} %get-tuple-element.53), channel_id=1, source_target_pairs={{0,4},{4,0},{8,12},{12,8},{16,20},{20,16},{24,28},{28,24},{1,5},{5... | collective-permute-start | bytes 196616 | tf_op jit(solution)/shard_map/ppermute | solution.py:467
  93.8 4.3 %collective-permute-start.14 = (f32[128,128]{1,0:T(8,128)S(1)}, f32[128,128]{1,0:T(8,128)S(1)}, u32[]{:S(2)}, u32[]{:S(2)}) collective-permute-start(f32[128,128]{1,0:T(8,128)S(1)} %add.94), channel_id=1, source_target_pairs={{0,8},{4,12},{8,0},{12,4},{16,24},{20,28},{24,16},{28,20},{1,9},{5... | collective-permute-start | bytes 196616 | tf_op jit(solution)/shard_map/ppermute | solution.py:467
  98.2 5.2 %collective-permute-start.15 = (f32[128,128]{1,0:T(8,128)S(1)}, f32[128,128]{1,0:T(8,128)S(1)}, u32[]{:S(2)}, u32[]{:S(2)}) collective-permute-start(f32[128,128]{1,0:T(8,128)S(1)} %add.95), channel_id=1, source_target_pairs={{0,16},{4,20},{8,24},{12,28},{16,0},{20,4},{24,8},{28,12},{1,17},{... | collective-permute-start | bytes 196616 | tf_op jit(solution)/shard_map/ppermute | solution.py:467
  107.8 2.9 %collective-permute-start.20 = (f32[128,128]{1,0:T(8,128)S(1)}, f32[128,128]{1,0:T(8,128)S(1)}, u32[]{:S(2)}, u32[]{:S(2)}) collective-permute-start(f32[128,128]{1,0:T(8,128)S(1)} %select_add_fusion), channel_id=1, source_target_pairs={{0,1},{4,5},{8,9},{12,13},{16,17},{20,21},{24,25},{28,29}} | collective-permute-start | bytes 196616 | tf_op jit(solution)/shard_map/ppermute | solution.py:543
  108.5 16.0 %collective-permute-start.17 = (f32[1024,128]{1,0:T(8,128)S(1)}, f32[1024,128]{1,0:T(8,128)S(1)}, u32[]{:S(2)}, u32[]{:S(2)}) collective-permute-start(f32[1024,128]{1,0:T(8,128)S(1)} %get-tuple-element.77), channel_id=1, source_target_pairs={{0,16},{2,18},{4,20},{6,22},{9,25},{11,27},{13,29},{15,31},{16,0},... | collective-permute-start | bytes 1572872 | tf_op jit(solution)/shard_map/ppermute | solution.py:492
  109.2 3.1 %collective-permute-start.18 = (f32[128,128]{1,0:T(8,128)S(1)}, f32[128,128]{1,0:T(8,128)S(1)}, u32[]{:S(2)}, u32[]{:S(2)}) collective-permute-start(f32[128,128]{1,0:T(8,128)S(1)} %add.96), channel_id=1, source_target_pairs={{0,1},{1,0},{2,3},{3,2},{4,5},{5,4},{6,7},{7,6},{8,9},{9,8},{10,11... | collective-permute-start | bytes 196616 | tf_op jit(solution)/shard_map/ppermute | solution.py:467
  110.7 6.7 %collective-permute-start.21 = (f32[128,128]{1,0:T(8,128)S(1)}, f32[128,128]{1,0:T(8,128)S(1)}, u32[]{:S(2)}, u32[]{:S(2)}) collective-permute-start(f32[128,128]{1,0:T(8,128)S(1)} %broadcast_select_fusion.1), channel_id=1, source_target_pairs={{0,2},{1,3},{4,6},{5,7},{8,10},{9,11},{12,14},{13,15},{16,18},{17,... | collective-permute-start | bytes 196616 | tf_op jit(solution)/shard_map/ppermute | solution.py:543
  112.3 12.2 %collective-permute-start.19 = (f32[128,128]{1,0:T(8,128)S(1)}, f32[128,128]{1,0:T(8,128)S(1)}, u32[]{:S(2)}, u32[]{:S(2)}) collective-permute-start(f32[128,128]{1,0:T(8,128)S(1)} %add.98), channel_id=1, source_target_pairs={{0,2},{1,3},{2,0},{3,1},{4,6},{5,7},{6,4},{7,5},{8,10},{9,11},{10,... | collective-permute-start | bytes 196616 | tf_op jit(solution)/shard_map/ppermute | solution.py:467
  125.0 6.9 %collective-permute-start.22 = (f32[1024,128]{1,0:T(8,128)S(1)}, f32[1024,128]{1,0:T(8,128)S(1)}, u32[]{:S(2)}, u32[]{:S(2)}) collective-permute-start(f32[1024,128]{1,0:T(8,128)S(1)} %collective-permute-done.17), channel_id=1, source_target_pairs={{0,2},{4,6},{9,11},{13,15},{18,16},{22,20},{27,25},{31,29}} | collective-permute-start | bytes 1572872 | tf_op jit(solution)/shard_map/ppermute | solution.py:516
  132.1 20.2 %collective-permute-start.23 = (f32[2048,128]{1,0:T(8,128)S(1)}, f32[2048,128]{1,0:T(8,128)S(1)}, u32[]{:S(2)}, u32[]{:S(2)}) collective-permute-start(f32[2048,128]{1,0:T(8,128)S(1)} %maximum_select_fusion.1.refs_3_), channel_id=1, source_target_pairs={{0,8},{2,10},{4,12},{6,14},{9,1},{11,3},{13,5},{15,7},{16,24},{18,... | collective-permute-start | bytes 3145736 | tf_op jit(solution)/shard_map/ppermute | solution.py:492
  133.4 36.0 %collective-permute-start.24 = (f32[2048,128]{1,0:T(8,128)S(1)}, f32[2048,128]{1,0:T(8,128)S(1)}, u32[]{:S(2)}, u32[]{:S(2)}) collective-permute-start(f32[2048,128]{1,0:T(8,128)S(1)} %maximum_select_fusion.1.refs_3_), channel_id=1, source_target_pairs={{0,4},{2,6},{4,0},{6,2},{9,13},{11,15},{13,9},{15,11},{16,20},{18,... | collective-permute-start | bytes 3145736 | tf_op jit(solution)/shard_map/ppermute | solution.py:492
  152.3 17.1 %collective-permute-start.25 = (f32[2048,128]{1,0:T(8,128)S(1)}, f32[2048,128]{1,0:T(8,128)S(1)}, u32[]{:S(2)}, u32[]{:S(2)}) collective-permute-start(f32[2048,128]{1,0:T(8,128)S(1)} %collective-permute-done.23.refs_4_), channel_id=1, source_target_pairs={{1,5},{3,7},{5,1},{7,3},{8,12},{10,14},{12,8},{14,10},{17,21},{19,... | collective-permute-start | bytes 3145736 | tf_op jit(solution)/shard_map/ppermute | solution.py:492
  (7 other events, 76.3 us)
